TPU v7x, 32 devices: a whole 2x2x4 slice. The times are simulated.
32 devices in a mesh: wave: 16 (over z, y, x), lev: 2 (over core).
Axes of the slice: x: 2, y: 2, z: 4, core: 2. Of those that a mesh axis runs over, the one named last changes fastest.
Arguments:
- spectra: bfloat16 [2, 3, 2, 1280, 1280], P('lev', None, None, None, 'wave'), may hold values from -0.119628906 to 0.119628906
- legendre: bfloat16 [1280, 16, 1280], P('wave'), may hold values from -0.15625 to 0.15625
- slot_wavenumbers: int32 [1280], replicated, may hold values from 0 to 1279, each once
- cycle_points: int32 [16], P('wave'), may hold values from 20 to 5136, as said below
- layer_depth_scaling: float32 [2], P('lev'), may hold values from 0.1 to 1
Outputs:
- physical_space_values: float32 [2, 16, 2, 3, 5376], P(None, 'wave', 'lev')
- height_potential_energy: float32 [2, 16, 2, 5376], P(None, 'wave', 'lev')
Inputs may be any that keep to these rules, and one draw needn't show every extreme that they name: `slot_wavenumbers`: each wavenumber stands in exactly one slot. `cycle_points`: each entry is 20 + 4 i for a latitude index i of 0 to 1279 counted from the pole; some entry has i = 1279.
All inputs are finite; a program needn't handle non-finite values.
Results may differ from a plain program's by a relative error of at most 0.0037.
Values may be sent and summed in bfloat16 or wider, within the bound.
No kernel may reach another device: no remote copies, remote signals or barrier semaphores. Data moves between devices by JAX's collectives and lax.ppermute only.
A program may use at most 128 MiB of HBM per device.

v0:
```python
import functools
import math

import jax
import jax.numpy as jnp
from jax import lax
from jax.experimental import pallas as pl
from jax.experimental.pallas import tpu as pltpu
from jax.sharding import PartitionSpec as P

PCOL = 5376
LANES = 128
FINE = 256
COARSE = PCOL // FINE
GROUP = 16
WIDE = 64
REST = 16
VMEM = 56 * 1024 * 1024


def cost(flops, size):
    return pl.CostEstimate(flops=flops, bytes_accessed=size, transcendentals=0)


def params():
    return pltpu.CompilerParams(vmem_limit_bytes=VMEM)


def block_rows(columns, slots):
    groups = columns * slots // GROUP
    return (groups // 2 + -(-groups // 8)) * GROUP


def pack_kernel(x_ref, o_ref):
    columns, _, rows = x_ref.shape
    targets = o_ref.shape[0]
    slots = rows // targets
    parts = slots // GROUP
    groups = columns * parts
    turned = [jnp.transpose(x_ref[c]) for c in range(columns)]
    for t in range(targets):
        base = t * slots
        for f in range(columns // 2):
            real = turned[2 * f][base : base + slots, :WIDE]
            imag = turned[2 * f + 1][base : base + slots, :WIDE]
            o_ref[t, f * slots : (f + 1) * slots, :] = jnp.concatenate([real, imag], 1)
        start = columns // 2 * slots
        for r in range(-(-groups // 8)):
            pieces = []
            for k in range(8):
                q = min(8 * r + k, groups - 1)
                c, s = q // parts, base + q % parts * GROUP
                pieces.append(turned[c][s : s + GROUP, WIDE:])
            o_ref[t, start + r * GROUP : start + (r + 1) * GROUP, :] = jnp.concatenate(pieces, 1)


def pack(x, targets):
    columns, degrees, rows = x.shape
    out_rows = block_rows(columns, rows // targets)
    return pl.pallas_call(
        pack_kernel,
        in_specs=[pl.BlockSpec(memory_space=pltpu.VMEM)],
        out_specs=pl.BlockSpec(memory_space=pltpu.VMEM),
        out_shape=jax.ShapeDtypeStruct((targets, out_rows, LANES), x.dtype),
        compiler_params=params(),
        cost_estimate=cost(0, 4_000_000),
        name="pack",
    )(x)


def basis_kernel(x_ref, m_ref, o_ref):
    group, lats, degrees = x_ref.shape
    width = group * lats
    x = x_ref[...].reshape(width, degrees)
    row = lax.broadcasted_iota(jnp.int32, (width, width), 0)
    column = lax.broadcasted_iota(jnp.int32, (width, width), 1)
    move = (row == column % group * lats + column // group).astype(jnp.float32).astype(x.dtype)
    turned = lax.dot_general(x, move, (((0,), (0,)), ((), ())), preferred_element_type=jnp.float32)
    degree = lax.broadcasted_iota(jnp.int32, (degrees, width), 0)
    live = jnp.where(degree >= m_ref[0], turned, 0.0).astype(o_ref.dtype)
    span = WIDE + REST
    sources = degrees // span
    for e in range(sources):
        o_ref[0, e * WIDE : (e + 1) * WIDE, :] = live[e * span : e * span + WIDE, :]
        to = sources * WIDE + e * REST
        o_ref[0, to : to + REST, :] = live[e * span + WIDE : (e + 1) * span, :]


def basis(legendre, waves):
    slots, lats, degrees = legendre.shape
    parts = slots // GROUP
    width = GROUP * lats
    return pl.pallas_call(
        basis_kernel,
        grid=(parts,),
        in_specs=[
            pl.BlockSpec((GROUP, lats, degrees), lambda i: (i, 0, 0)),
            pl.BlockSpec((1, 1, width), lambda i: (i, 0, 0)),
        ],
        out_specs=pl.BlockSpec((1, degrees, width), lambda i: (i, 0, 0)),
        out_shape=jax.ShapeDtypeStruct((parts, degrees, width), legendre.dtype),
        compiler_params=params(),
        cost_estimate=cost(2 * slots * lats * degrees * 256, 7_000_000),
        name="basis",
    )(legendre, waves)


def section_kernel(copies, r_ref, b_ref, m_ref, _, scale_ref, o_ref, s_ref):
    sources = r_ref.shape[0]
    parts, degrees, width = b_ref.shape
    lats = width // GROUP
    columns = s_ref.shape[0] // (2 * GROUP)
    slots = parts * GROUP
    half = columns * GROUP
    start = columns // 2 * slots
    sign = 1.0 - 2.0 * (lax.broadcasted_iota(jnp.int32, (half, degrees), 1) % 2).astype(jnp.float32)
    sign = sign.astype(s_ref.dtype)
    row = lax.broadcasted_iota(jnp.int32, (2 * half, width), 0)
    lane = lax.broadcasted_iota(jnp.int32, (2 * half, width), 1)
    same = row % GROUP == lane % GROUP
    fields = columns // 2
    pick_row = lax.broadcasted_iota(jnp.int32, (16, 2 * half), 0)
    pick_lane = lax.broadcasted_iota(jnp.int32, (16, 2 * half), 1)
    part, place = pick_row // 8, pick_row % 8
    spare = place >= 2 * fields
    hemisphere = jnp.where(spare, place - 2 * fields, place // fields)
    field = jnp.where(spare, 0, place % fields)
    pick = pick_lane // GROUP == hemisphere * columns + field * 2 + part
    pick = pick.astype(jnp.float32).astype(s_ref.dtype)
    out_row = lax.broadcasted_iota(jnp.int32, (16, width), 0) % 8
    south = ((out_row >= fields) & (out_row < 2 * fields)) | (out_row == 2 * fields + 1)
    rows = []
    for g in range(parts):
        for c in range(columns):
            at = c // 2 * slots + g * GROUP
            lo = c % 2 * WIDE
            q = c * parts + g
            rest_at, rest_lo = start + q // 8 * GROUP, q % 8 * REST
            to = slice(c * GROUP, (c + 1) * GROUP)
            wide = [r_ref[e, at : at + GROUP, lo : lo + WIDE] for e in range(sources)]
            rest = [r_ref[e, rest_at : rest_at + GROUP, rest_lo : rest_lo + REST] for e in range(sources)]
            s_ref[to, :] = jnp.concatenate(wide + rest, 1)
        s_ref[half:, :] = s_ref[:half, :] * sign
        sums = jnp.dot(s_ref[...], b_ref[g], preferred_element_type=jnp.float32)
        own = jnp.where(same, sums, 0.0).astype(s_ref.dtype)
        found = jnp.dot(pick, own, preferred_element_type=jnp.float32)
        parity = (1 - 2 * (m_ref[g] % 2)).astype(jnp.float32)
        rows.append(jnp.where(south, found * parity, found))
    blank = jnp.zeros((16, LANES - slots), jnp.float32)
    for l in range(lats):
        pieces = [r[:, l * GROUP : (l + 1) * GROUP] for r in rows] + [blank]
        tile = jnp.concatenate(pieces, 1).astype(o_ref.dtype)
        for v in range(copies):
            o_ref[l, v] = tile


def section(received, table, waves, ready, scales, columns, copies):
    parts, degrees, width = table.shape
    lats = width // GROUP
    return pl.pallas_call(
        functools.partial(section_kernel, copies),
        in_specs=[pl.BlockSpec(memory_space=pltpu.VMEM)] * 3
        + [pl.BlockSpec(memory_space=pl.ANY), pl.BlockSpec(memory_space=pltpu.SMEM)],
        out_specs=pl.BlockSpec(memory_space=pltpu.VMEM),
        out_shape=jax.ShapeDtypeStruct((lats, copies, 16, LANES), received.dtype),
        scratch_shapes=[pltpu.VMEM((2 * columns * GROUP, degrees), received.dtype)],
        compiler_params=params(),
        cost_estimate=cost(10_000_000_000, 4_000_000),
        name="section",
    )(received, table, waves, ready, scales)


def plain_section(received, legendre, waves, copies):
    columns, slots, degrees = received.shape
    fields = columns // 2
    degree = lax.broadcasted_iota(jnp.int32, (slots, degrees), 1)
    live = degree >= waves[:, None]
    odd = (degree + waves[:, None]) % 2 == 1
    blank = jnp.zeros_like(received)
    north = jnp.where(live[None], received, blank)
    south = jnp.where(odd[None], -north, north)
    both = jnp.stack([north, south], 0).reshape(2, fields, 2, slots, degrees)
    sums = jnp.einsum("sln,hfisn->lihfs", legendre, both, preferred_element_type=jnp.float32)
    lats = legendre.shape[1]
    rows = jnp.concatenate([sums.reshape(lats, 2, 2 * fields, slots), sums[:, :, :, 0]], 2)
    rows = rows.reshape(lats, 16, slots).astype(received.dtype)
    rows = jnp.pad(rows, ((0, 0), (0, 0), (0, LANES - slots)))
    return jnp.broadcast_to(rows[:, None], (lats, copies, 16, LANES))


def turn(product, points):
    inverse = 1.0 / points
    whole = jnp.floor(product * inverse + 0.5)
    residue = product - whole * points
    quarter = jnp.floor(4.0 * residue * inverse + 0.5)
    small = (4.0 * residue - quarter * points) * inverse * (0.5 * math.pi)
    square = small * small
    sine = small * (1.0 + square * (-1.0 / 6 + square * (1.0 / 120 + square * (-1.0 / 5040))))
    cosine = 1.0 + square * (-0.5 + square * (1.0 / 24 + square * (-1.0 / 720 + square * (1.0 / 40320))))
    which = quarter.astype(jnp.int32) & 3
    swap = (which & 1) == 1
    first = jnp.where(swap, sine, cosine)
    second = jnp.where(swap, cosine, sine)
    first = jnp.where((which == 1) | (which == 2), -first, first)
    second = jnp.where(which >= 2, -second, second)
    return first, second


def table_kernel(points_ref, m_ref, t_ref, c_ref, s_ref):
    points = points_ref[0].astype(jnp.float32)
    m = m_ref[0].astype(jnp.float32)
    down = jnp.transpose(jnp.broadcast_to(m, (LANES, LANES)))
    down = jnp.concatenate([down] * (FINE // LANES), 1)
    point = lax.broadcasted_iota(jnp.int32, (LANES, FINE), 1).astype(jnp.float32)
    cosine, sine = turn(down * point, points)
    t_ref[0] = cosine.astype(t_ref.dtype)
    t_ref[1] = (-sine).astype(t_ref.dtype)
    coarse = lax.broadcasted_iota(jnp.int32, c_ref.shape, 0) * FINE
    cosine, sine = turn(m * coarse.astype(jnp.float32), points)
    share = jnp.where(m == 0.0, 1.0, 2.0)
    c_ref[...] = cosine * share
    s_ref[...] = sine * share


def tables(points, slot_waves):
    sources = slot_waves.shape[0]
    depth = sources * LANES
    steps = -(-COARSE // 8) * 8
    return pl.pallas_call(
        table_kernel,
        grid=(sources,),
        in_specs=[
            pl.BlockSpec(memory_space=pltpu.SMEM),
            pl.BlockSpec((1, 1, LANES), lambda i: (i, 0, 0)),
        ],
        out_specs=[
            pl.BlockSpec((2, LANES, FINE), lambda i: (0, i, 0)),
            pl.BlockSpec((steps, LANES), lambda i: (0, i)),
            pl.BlockSpec((steps, LANES), lambda i: (0, i)),
        ],
        out_shape=[
            jax.ShapeDtypeStruct((2, depth, FINE), jnp.bfloat16),
            jax.ShapeDtypeStruct((steps, depth), jnp.float32),
            jax.ShapeDtypeStruct((steps, depth), jnp.float32),
        ],
        compiler_params=params(),
        cost_estimate=cost(60_000_000, 3_000_000),
        name="tables",
    )(points, slot_waves)


def synth_kernel(points_ref, place_ref, scale_ref, r_ref, t_ref, c_ref, s_ref, v_ref, h_ref, g_ref):
    sources, levels = r_ref.shape[:2]
    depth = sources * LANES
    me = place_ref[0]
    fields = v_ref.shape[1]
    row = lax.broadcasted_iota(jnp.int32, (16, LANES), 0) % 8
    spare = row >= 2 * fields
    weights = []
    for v in range(levels):
        summed = jnp.where(v >= me, scale_ref[v], 0.0)
        single = jnp.where(v == me, 1.0, 0.0)
        weights.append(jnp.where(spare, summed, single))

    def fill(e, carry):
        rows = sum(weights[v] * r_ref[e, v].astype(jnp.float32) for v in range(levels))
        real, imag = rows[:8], rows[8:]
        lanes = pl.ds(pl.multiple_of(e * LANES, LANES), LANES)
        shifted = pl.ds(pl.multiple_of(depth + e * LANES, LANES), LANES)
        for pair in range(g_ref.shape[0] // 16):
            first, second = [], []
            for b in (2 * pair, 2 * pair + 1):
                cosine, sine = c_ref[b : b + 1, lanes], s_ref[b : b + 1, lanes]
                first.append(real * cosine - imag * sine)
                second.append(real * sine + imag * cosine)
            to = slice(pair * 16, pair * 16 + 16)
            g_ref[to, lanes] = jnp.concatenate(first, 0).astype(g_ref.dtype)
            g_ref[to, shifted] = jnp.concatenate(second, 0).astype(g_ref.dtype)
        return carry

    lax.fori_loop(0, sources, fill, 0)
    table = t_ref[...].reshape(2 * depth, FINE)
    values = jnp.dot(g_ref[...], table, preferred_element_type=jnp.float32)
    lane = lax.broadcasted_iota(jnp.int32, (8, FINE), 1)
    for b in range(COARSE):
        at = slice(b * FINE, (b + 1) * FINE)
        part = jnp.where(lane + b * FINE < points_ref[0], values[8 * b : 8 * b + 8], 0.0)
        for h in range(2):
            for f in range(fields):
                v_ref[h, f, :, at] = part[h * fields + f : h * fields + f + 1]
            h_ref[h, 0, :, at] = part[2 * fields + h : 2 * fields + h + 1]


def synthesis(points, place, scales, received, table, cosine, sine, fields):
    depth = received.shape[0] * LANES
    smem, vmem = pl.BlockSpec(memory_space=pltpu.SMEM), pl.BlockSpec(memory_space=pltpu.VMEM)
    return pl.pallas_call(
        synth_kernel,
        in_specs=[smem] * 3 + [vmem] * 4,
        out_specs=[vmem] * 2,
        out_shape=[
            jax.ShapeDtypeStruct((2, fields, 1, PCOL), jnp.float32),
            jax.ShapeDtypeStruct((2, 1, 1, PCOL), jnp.float32),
        ],
        scratch_shapes=[pltpu.VMEM(((COARSE + 1) // 2 * 16, 2 * depth), jnp.bfloat16)],
        compiler_params=params(),
        cost_estimate=cost(1_000_000_000, 3_000_000),
        name="synth",
    )(points, place, scales, received, table, cosine, sine)


def shards(spectra, legendre, slot_wavenumbers, cycle_points, layer_depth_scaling):
    slots, lats, degrees = legendre.shape
    levels_here, fields = spectra.shape[:2]
    assert levels_here == 1 and cycle_points.shape[0] == 1 and fields == 3
    waves, levels = lax.axis_size("wave"), lax.axis_size("lev")
    columns = fields * 2
    own = lax.dynamic_slice_in_dim(slot_wavenumbers, lax.axis_index("wave") * slots, slots)
    x = spectra.reshape(columns, waves * slots, spectra.shape[4])
    slot_waves = jnp.pad(slot_wavenumbers.reshape(waves, slots), ((0, 0), (0, LANES - slots)))
    table, cosine, sine = tables(cycle_points, slot_waves.reshape(waves, 1, LANES))
    scales = lax.all_gather(layer_depth_scaling, "lev", tiled=True)
    place = lax.axis_index("lev").reshape(1)
    if spectra.shape[4] == WIDE + REST and slots % GROUP == 0 and lats == 16:
        parts = slots // GROUP
        spread = jnp.broadcast_to(own.reshape(parts, 1, GROUP), (parts, lats, GROUP))
        spread = spread.reshape(parts, 1, lats * GROUP)
        sent = pack(jnp.swapaxes(x, 1, 2), waves)
        received = lax.all_to_all(sent, "wave", 0, 0, tiled=True)
        rows = section(received, basis(legendre, spread), spread, cosine, scales, columns, levels)
    else:
        received = lax.all_to_all(x, "wave", split_axis=1, concat_axis=2, tiled=True)
        rows = plain_section(received, legendre, own, levels)
    rows = rows.reshape(waves * levels, 16, LANES)
    rows = lax.all_to_all(rows, ("wave", "lev"), 0, 0, tiled=True)
    rows = rows.reshape(waves, levels, 16, LANES)
    values, height = synthesis(cycle_points, place, scales, rows, table, cosine, sine, fields)
    return jnp.transpose(values, (0, 2, 1, 3))[:, :, None], height


def solution(mesh):
    in_specs = (P("lev", None, None, None, "wave"), P("wave", None, None), P(), P("wave"), P("lev"))
    out_specs = (P(None, "wave", "lev", None, None), P(None, "wave", "lev", None))
    call = jax.shard_map(shards, mesh=mesh, in_specs=in_specs, out_specs=out_specs, check_vma=False)

    def whole(*arrays):
        values, height = call(*arrays)
        return values, height

    return whole
```

profile of v0, /device:TPU:0, one launch (start us, length us, event | category | flops | bytes accessed | tf_op | source)
XLA Modules:
  0.0 64.4 jit_solution(15127394226858596634)
XLA Ops:
  0.6 0.0 copy-start.3
  0.6 0.0 copy-start.2
  0.7 3.7 %pack.1 = bf16[16,304,128]{2,1,0:T(8,128)(2,1)} custom-call(bf16[6,80,1280]{2,1,0:T(8,128)(2,1)} %bitcast.11), custom_call_target="tpu_custom_call" | custom-call | bytes 4000000 | tf_op jit(solution)/shard_map/pack/pallas_call | solution.py:60
  4.3 8.3 %all-to-all-start = ((bf16[16,304,128]{2,1,0:T(8,128)(2,1)}), bf16[16,304,128]{2,1,0:T(8,128)(2,1)S(1)}, u32[]{:S(2)}, u32[]{:S(2)}) async-start(bf16[16,304,128]{2,1,0:T(8,128)(2,1)} %pack.1), calls=%async_computation | async-start | bytes 2490368 | tf_op jit(solution)/shard_map/all_to_all | solution.py:329
  13.3 0.0 copy-done.3
  13.3 0.6 dynamic-slice
  13.9 0.8 %dynamic-update-slice = f32[2]{0:T(128)S(1)} dynamic-update-slice(f32[2]{0:T(128)S(1)} %broadcast.2, f32[1]{0:T(128)S(6)} %copy.10, u32[]{:T(128)} %bitcast.1) | dynamic-update-slice | bytes 12
  14.6 3.0 %all-reduce.1.scale_ref = f32[2]{0:T(128)} all-reduce(f32[2]{0:T(128)S(1)} %dynamic-update-slice), channel_id=1, replica_groups=mesh['wave'=16,'lev'=2] {'lev'}, use_global_device_ids=true, to_apply=%add.1 | all-reduce | flops 2 | bytes 16
  18.3 0.0 copy-done.2
  18.3 0.1 reshape.30
  18.4 0.1 dynamic_slice.3
  18.5 0.1 broadcast_in_dim.7
  18.5 0.6 pad.4
  19.1 0.7 %reshape.29.m_ref = s32[5,1,256]{2,1,0:T(1,128)} reshape(s32[5,16,16]{2,1,0:T(8,128)S(1)} %broadcast_in_dim.8) | data formatting | bytes 10240 | tf_op jit(solution)/shard_map/reshape | solution.py:327
  19.8 9.6 %tables.1 = (bf16[2,2048,256]{2,1,0:T(8,128)(2,1)}, f32[24,2048]{1,0:T(8,128)}, f32[24,2048]{1,0:T(8,128)}) custom-call(s32[1]{0:T(128)S(6)} %copy.9.points_ref, s32[16,1,128]{2,1,0:T(1,128)} %bitcast.14), custom_call_target="tpu_custom_call" | custom-call | flops 60000000 | bytes 3000000 | tf_op jit(solution)/shard_map/tables/pallas_call | solution.py:229
  29.4 5.9 %basis.1.b_ref = bf16[5,1280,256]{2,1,0:T(8,128)(2,1)} custom-call(bf16[80,16,1280]{2,1,0:T(8,128)(2,1)} %x_ref.1, s32[5,1,256]{2,1,0:T(1,128)} %reshape.29.m_ref), custom_call_target="tpu_custom_call" | custom-call | flops 838860800 | bytes 7000000 | tf_op jit(solution)/shard_map/basis/pallas_call | solution.py:93
  35.3 5.6 %all-to-all-done.r_ref = bf16[16,304,128]{2,1,0:T(8,128)(2,1)S(1)} async-done(((bf16[16,304,128]{2,1,0:T(8,128)(2,1)}), bf16[16,304,128]{2,1,0:T(8,128)(2,1)S(1)}, u32[]{:S(2)}, u32[]{:S(2)}) %all-to-all-start) | async-done | bytes 1245216 | tf_op jit(solution)/shard_map/all_to_all | solution.py:329
  40.9 0.0 copy-start
  40.9 1.1 %copy-done = bf16[16,304,128]{2,1,0:T(8,128)(2,1)} copy-done((bf16[16,304,128]{2,1,0:T(8,128)(2,1)}, bf16[16,304,128]{2,1,0:T(8,128)(2,1)S(1)}, u32[]{:S(2)}) %copy-start) | copy-done | bytes 1245208
  41.9 4.8 %section.1 = bf16[16,2,16,128]{3,2,1,0:T(8,128)(2,1)} custom-call(bf16[16,304,128]{2,1,0:T(8,128)(2,1)} %copy-done, bf16[5,1280,256]{2,1,0:T(8,128)(2,1)} %basis.1.b_ref, s32[5,1,256]{2,1,0:T(1,128)} %reshape.29.m_ref, f32[24,2048]{1,0:T(8,128)} %get-tuple-element.7._.c_ref, f32[2]{0:T(128)} %all-reduce.1.scale_ref), custom_call_target="tpu_custom_call" | custom-call | flops 10000000000 | bytes 4000000 | tf_op jit(solution)/shard_map/section/pallas_call | solution.py:160
  46.8 5.3 %all-to-all-start.1 = ((bf16[32,16,128]{2,1,0:T(8,128)(2,1)}), bf16[32,16,128]{2,1,0:T(8,128)(2,1)S(1)}, u32[]{:S(2)}, u32[]{:S(2)}) async-start(bf16[32,16,128]{2,1,0:T(8,128)(2,1)} %bitcast.13), calls=%async_computation.1 | async-start | bytes 262144 | tf_op jit(solution)/shard_map/all_to_all | solution.py:335
  52.1 8.2 %all-to-all-done.1 = bf16[32,16,128]{2,1,0:T(8,128)(2,1)S(1)} async-done(((bf16[32,16,128]{2,1,0:T(8,128)(2,1)}), bf16[32,16,128]{2,1,0:T(8,128)(2,1)S(1)}, u32[]{:S(2)}, u32[]{:S(2)}) %all-to-all-start.1) | async-done | bytes 131104 | tf_op jit(solution)/shard_map/all_to_all | solution.py:335
  60.3 0.0 copy-start.1
  60.3 0.7 %copy-done.1 = bf16[32,16,128]{2,1,0:T(8,128)(2,1)} copy-done((bf16[32,16,128]{2,1,0:T(8,128)(2,1)}, bf16[32,16,128]{2,1,0:T(8,128)(2,1)S(1)}, u32[]{:S(2)}) %copy-start.1) | copy-done | bytes 131096
  60.9 3.4 %synth.1 = (f32[2,3,1,5376]{3,2,1,0:T(1,128)}, f32[2,1,1,5376]{3,2,1,0:T(1,128)}) custom-call(s32[1]{0:T(128)S(6)} %copy.9.points_ref, s32[1]{0:T(128)} %bitcast.place_ref, f32[2]{0:T(128)} %all-reduce.1.scale_ref, bf16[16,2,16,128]{3,2,1,0:T(8,128)(2,1)} %bitcast.12, bf16[2,2048,256]{2,1,0:T(8,128)(2,1)} %get-tuple-element.8.t_ref, ...), custom_call_target="tpu_custom_call" | custom-call | flops 1000000000 | bytes 3000000 | tf_op jit(solution)/shard_map/synth/pallas_call | solution.py:297
  (2 shorter events, 0.0 us)
Async XLA Ops:
  0.6 12.7 %copy-start.3 = (u32[32]{0:T(128)S(1)}, u32[32]{0:T(128)}, u32[]{:S(2)}) copy-start(u32[32]{0:T(128)} %constant.21) | copy-start | bytes 388
  0.6 17.7 %copy-start.2 = (s32[1280]{0:T(1024)S(1)}, s32[1280]{0:T(1024)}, u32[]{:S(2)}) copy-start(s32[1280]{0:T(1024)} %param.7) | copy-start | bytes 15364
  4.3 36.6 %all-to-all-start = ((bf16[16,304,128]{2,1,0:T(8,128)(2,1)}), bf16[16,304,128]{2,1,0:T(8,128)(2,1)S(1)}, u32[]{:S(2)}, u32[]{:S(2)}) async-start(bf16[16,304,128]{2,1,0:T(8,128)(2,1)} %pack.1), calls=%async_computation | async-start | bytes 2490368 | tf_op jit(solution)/shard_map/all_to_all | solution.py:329
  40.9 1.1 %copy-start = (bf16[16,304,128]{2,1,0:T(8,128)(2,1)}, bf16[16,304,128]{2,1,0:T(8,128)(2,1)S(1)}, u32[]{:S(2)}) copy-start(bf16[16,304,128]{2,1,0:T(8,128)(2,1)S(1)} %all-to-all-done.r_ref) | copy-start | bytes 3735556
  46.8 13.5 %all-to-all-start.1 = ((bf16[32,16,128]{2,1,0:T(8,128)(2,1)}), bf16[32,16,128]{2,1,0:T(8,128)(2,1)S(1)}, u32[]{:S(2)}, u32[]{:S(2)}) async-start(bf16[32,16,128]{2,1,0:T(8,128)(2,1)} %bitcast.13), calls=%async_computation.1 | async-start | bytes 262144 | tf_op jit(solution)/shard_map/all_to_all | solution.py:335
  60.3 0.7 %copy-start.1 = (bf16[32,16,128]{2,1,0:T(8,128)(2,1)}, bf16[32,16,128]{2,1,0:T(8,128)(2,1)S(1)}, u32[]{:S(2)}) copy-start(bf16[32,16,128]{2,1,0:T(8,128)(2,1)S(1)} %all-to-all-done.1) | copy-start | bytes 393220
where the time goes:
time: 65 us; the launch traced here: 64.4 us
  Pallas kernels  27.4 us (42%)
  waiting for transfers between devices  13.8 us (21%)
  starting transfers between devices  13.6 us (21%)
  local copies, waits for them, and re-layouts  4.61 us (7%)
  blocking collectives  3.01 us (5%)
  between operations  2 us (3%)
    pallas_call x1, Pallas kernels, tables(): pl.pallas_call(table_kernel, grid=(sources,), in_specs=[pl.BlockSpec(memo...  9.58 us
    all_to_all x1, starting transfers between devices, shards(): received = lax.all_to_all(sent, 'wave', 0, 0, tiled=True)  8.31 us
    all_to_all x1, waiting for transfers between devices, shards(): rows = lax.all_to_all(rows, ('wave', 'lev'), 0, 0, tiled=True)  8.22 us
    pallas_call x1, Pallas kernels, basis(): pl.pallas_call(basis_kernel, grid=(parts,), in_specs=[pl.BlockSpec((GROUP...  5.87 us
    all_to_all x1, waiting for transfers between devices, shards(): received = lax.all_to_all(sent, 'wave', 0, 0, tiled=True)  5.59 us
    all_to_all x1, starting transfers between devices, shards(): rows = lax.all_to_all(rows, ('wave', 'lev'), 0, 0, tiled=True)  5.26 us
    pallas_call x1, Pallas kernels, section(): pl.pallas_call(functools.partial(section_kernel, copies), in_specs=[pl.Bl...  4.84 us
    pallas_call x1, Pallas kernels, pack(): pl.pallas_call(pack_kernel, in_specs=[pl.BlockSpec(memory_space=pltpu.VME...  3.65 us
  transfers between devices with their start and end apart: 2, of which 2 were waited for; matrix products, arithmetic and copies ran while one was open for 4% of the time, Pallas kernels for 24%

commit v1 on v0

v1 whole, which is shorter than its diff:
```python
import functools
import math

import jax
import jax.numpy as jnp
from jax import lax
from jax.experimental import pallas as pl
from jax.experimental.pallas import tpu as pltpu
from jax.sharding import PartitionSpec as P

PCOL = 5376
LANES = 128
FINE = 256
COARSE = PCOL // FINE
GROUP = 16
WIDE = 64
REST = 16


def cost(flops, size):
    return pl.CostEstimate(flops=flops, bytes_accessed=size, transcendentals=0)


def params(size=16):
    return pltpu.CompilerParams(vmem_limit_bytes=size * 1024 * 1024)


def block_rows(columns, slots):
    groups = columns * slots // GROUP
    return (groups // 2 + -(-groups // 8)) * GROUP


def pack_kernel(x_hbm, o_hbm, x_ref, o_ref, in_sems, out_sems):
    columns, _, rows = x_ref.shape
    targets = o_ref.shape[0]
    slots = rows // targets
    parts = slots // GROUP
    groups = columns * parts
    loads, stores = [], []
    for i in range(2):
        some = pl.ds(i * columns // 2, columns // 2)
        loads.append(pltpu.make_async_copy(x_hbm.at[some], x_ref.at[some], in_sems.at[i]))
        loads[i].start()
    turned = []
    for c in range(columns):
        if c % (columns // 2) == 0:
            loads[c // (columns // 2)].wait()
        turned.append(jnp.transpose(x_ref[c]))
    chunk = targets // 4
    for t in range(targets):
        base = t * slots
        for g in range(parts):
            s = slice(base + g * GROUP, base + (g + 1) * GROUP)
            for f in range(columns // 2):
                at = (g * columns // 2 + f) * GROUP
                real, imag = turned[2 * f][s, :WIDE], turned[2 * f + 1][s, :WIDE]
                o_ref[t, at : at + GROUP, :] = jnp.concatenate([real, imag], 1)
        start = columns // 2 * slots
        for r in range(-(-groups // 8)):
            pieces = []
            for k in range(8):
                q = min(8 * r + k, groups - 1)
                s = base + q // columns * GROUP
                pieces.append(turned[q % columns][s : s + GROUP, WIDE:])
            o_ref[t, start + r * GROUP : start + (r + 1) * GROUP, :] = jnp.concatenate(pieces, 1)
        if (t + 1) % chunk == 0:
            i = t // chunk
            some = pl.ds(i * chunk, chunk)
            stores.append(pltpu.make_async_copy(o_ref.at[some], o_hbm.at[some], out_sems.at[i]))
            stores[i].start()
    for store in stores:
        store.wait()


def pack(x, targets):
    columns, degrees, rows = x.shape
    out = (targets, block_rows(columns, rows // targets), LANES)
    return pl.pallas_call(
        pack_kernel,
        in_specs=[pl.BlockSpec(memory_space=pl.ANY)],
        out_specs=pl.BlockSpec(memory_space=pl.ANY),
        out_shape=jax.ShapeDtypeStruct(out, x.dtype),
        scratch_shapes=[
            pltpu.VMEM(x.shape, x.dtype),
            pltpu.VMEM(out, x.dtype),
            pltpu.SemaphoreType.DMA((2,)),
            pltpu.SemaphoreType.DMA((4,)),
        ],
        compiler_params=params(56),
        cost_estimate=cost(0, 4_000_000),
        name="pack",
    )(x)


def section_kernel(copies, r_hbm, x_ref, m_ref, *rest):
    o_ref, r_ref, s_ref, f_ref, sem = rest[-5:]
    sources = r_ref.shape[0]
    slots, lats, degrees = x_ref.shape
    parts = slots // GROUP
    width = GROUP * lats
    columns = s_ref.shape[1] // (2 * GROUP)
    fields = columns // 2
    half = columns * GROUP
    start = columns // 2 * slots
    arrive = pltpu.make_async_copy(r_hbm, r_ref, sem)
    arrive.start()
    row = lax.broadcasted_iota(jnp.int32, (2 * half, width), 0)
    lane = lax.broadcasted_iota(jnp.int32, (2 * half, width), 1)
    same = (row % GROUP == lane // lats).reshape(2 * columns, GROUP, width)
    degree = lax.broadcasted_iota(jnp.int32, (GROUP, degrees), 1)
    arrive.wait()
    for g in range(parts):
        wave = m_ref[g * GROUP : (g + 1) * GROUP, :]
        live = degree >= wave
        sign = (1 - 2 * ((degree + wave) % 2)).astype(jnp.float32)
        north = jnp.where(live, 1.0, 0.0).astype(s_ref.dtype)
        south = jnp.where(live, sign, 0.0).astype(s_ref.dtype)
        for c in range(columns):
            at = (g * columns // 2 + c // 2) * GROUP
            lo = c % 2 * WIDE
            q = g * columns + c
            rest_at, rest_lo = start + q // 8 * GROUP, q % 8 * REST
            pieces = []
            for e in range(sources):
                pieces.append(r_ref[e, at : at + GROUP, lo : lo + WIDE])
                pieces.append(r_ref[e, rest_at : rest_at + GROUP, rest_lo : rest_lo + REST])
            tile = jnp.concatenate(pieces, 1)
            to = (c % 2 * 2 * fields + c // 2) * GROUP
            s_ref[g, to : to + GROUP, :] = tile * north
            to += fields * GROUP
            s_ref[g, to : to + GROUP, :] = tile * south
        basis = x_ref[g * GROUP : (g + 1) * GROUP].reshape(width, degrees)
        sums = lax.dot_general(
            s_ref[g], basis, (((1,), (1,)), ((), ())), preferred_element_type=jnp.float32
        )
        found = jnp.sum(jnp.where(same, sums.reshape(same.shape), 0.0), axis=1)
        for i in range(2):
            at, first = g * 16 + 8 * i, 2 * fields * i
            f_ref[at : at + 2 * fields, :] = found[first : first + 2 * fields]
            f_ref[at + 2 * fields : at + 2 * fields + 1, :] = found[first : first + 1]
            f_ref[at + 2 * fields + 1 : at + 8, :] = found[first + fields : first + fields + 1]
    source = lax.broadcasted_iota(jnp.int32, (width, width), 0)
    target = lax.broadcasted_iota(jnp.int32, (width, width), 1)
    move = (target == source % lats * GROUP + source // lats).astype(jnp.float32).astype(s_ref.dtype)
    moved = jnp.dot(f_ref[...].astype(s_ref.dtype), move, preferred_element_type=jnp.float32)
    blank = jnp.zeros((16, LANES - slots), jnp.float32)
    for l in range(lats):
        pieces = [moved[g * 16 : (g + 1) * 16, l * GROUP : (l + 1) * GROUP] for g in range(parts)]
        tile = jnp.concatenate(pieces + [blank], 1).astype(o_ref.dtype)
        for v in range(copies):
            o_ref[l, v] = tile


def section(received, legendre, waves, ready, columns, copies):
    slots, lats, degrees = legendre.shape
    parts = slots // GROUP
    spaces = [pl.ANY, pltpu.VMEM, pltpu.VMEM] + [pl.ANY] * len(ready)
    return pl.pallas_call(
        functools.partial(section_kernel, copies),
        in_specs=[pl.BlockSpec(memory_space=space) for space in spaces],
        out_specs=pl.BlockSpec(memory_space=pltpu.VMEM),
        out_shape=jax.ShapeDtypeStruct((lats, copies, 16, LANES), received.dtype),
        scratch_shapes=[
            pltpu.VMEM(received.shape, received.dtype),
            pltpu.VMEM((parts, 2 * columns * GROUP, degrees), received.dtype),
            pltpu.VMEM((parts * 16, GROUP * lats), jnp.float32),
            pltpu.SemaphoreType.DMA,
        ],
        compiler_params=params(),
        cost_estimate=cost(10_000_000_000, 4_000_000),
        name="section",
    )(received, legendre, waves, *ready)


def plain_section(received, legendre, waves, copies):
    columns, slots, degrees = received.shape
    fields = columns // 2
    degree = lax.broadcasted_iota(jnp.int32, (slots, degrees), 1)
    live = degree >= waves[:, None]
    odd = (degree + waves[:, None]) % 2 == 1
    blank = jnp.zeros_like(received)
    north = jnp.where(live[None], received, blank)
    south = jnp.where(odd[None], -north, north)
    both = jnp.stack([north, south], 0).reshape(2, fields, 2, slots, degrees)
    sums = jnp.einsum("sln,hfisn->lihfs", legendre, both, preferred_element_type=jnp.float32)
    lats = legendre.shape[1]
    rows = jnp.concatenate([sums.reshape(lats, 2, 2 * fields, slots), sums[:, :, :, 0]], 2)
    rows = rows.reshape(lats, 16, slots).astype(received.dtype)
    rows = jnp.pad(rows, ((0, 0), (0, 0), (0, LANES - slots)))
    return jnp.broadcast_to(rows[:, None], (lats, copies, 16, LANES))


def turn(product, points):
    inverse = 1.0 / points
    whole = jnp.floor(product * inverse + 0.5)
    residue = product - whole * points
    quarter = jnp.floor(4.0 * residue * inverse + 0.5)
    small = (4.0 * residue - quarter * points) * inverse * (0.5 * math.pi)
    square = small * small
    sine = small * (1.0 + square * (-1.0 / 6 + square * (1.0 / 120 + square * (-1.0 / 5040))))
    cosine = 1.0 + square * (-0.5 + square * (1.0 / 24 + square * (-1.0 / 720 + square * (1.0 / 40320))))
    which = quarter.astype(jnp.int32) & 3
    swap = (which & 1) == 1
    first = jnp.where(swap, sine, cosine)
    second = jnp.where(swap, cosine, sine)
    first = jnp.where((which == 1) | (which == 2), -first, first)
    second = jnp.where(which >= 2, -second, second)
    return first, second


def table_kernel(points_ref, m_ref, _, t_ref, c_ref, s_ref, done_ref):
    done_ref[...] = jnp.zeros_like(done_ref)
    points = points_ref[0].astype(jnp.float32)
    m = m_ref[...].astype(jnp.float32)
    down = jnp.transpose(jnp.broadcast_to(m, (LANES, LANES)))
    down = jnp.concatenate([down] * (FINE // LANES), 1)
    point = lax.broadcasted_iota(jnp.int32, (LANES, FINE), 1).astype(jnp.float32)
    cosine, sine = turn(down * point, points)
    t_ref[0] = cosine.astype(t_ref.dtype)
    t_ref[1] = (-sine).astype(t_ref.dtype)
    coarse = lax.broadcasted_iota(jnp.int32, c_ref.shape, 0) * FINE
    cosine, sine = turn(m * coarse.astype(jnp.float32), points)
    share = jnp.where(m == 0.0, 1.0, 2.0)
    c_ref[...] = cosine * share
    s_ref[...] = sine * share


def tables(points, slot_waves, early):
    depth = slot_waves.shape[1]
    steps = -(-COARSE // 8) * 8
    return pl.pallas_call(
        table_kernel,
        grid=(depth // LANES,),
        in_specs=[
            pl.BlockSpec(memory_space=pltpu.SMEM),
            pl.BlockSpec((1, LANES), lambda i: (0, i)),
            pl.BlockSpec(memory_space=pl.ANY),
        ],
        out_specs=[
            pl.BlockSpec((2, LANES, FINE), lambda i: (0, i, 0)),
            pl.BlockSpec((steps, LANES), lambda i: (0, i)),
            pl.BlockSpec((steps, LANES), lambda i: (0, i)),
            pl.BlockSpec((8, LANES), lambda i: (0, 0)),
        ],
        out_shape=[
            jax.ShapeDtypeStruct((2, depth, FINE), jnp.bfloat16),
            jax.ShapeDtypeStruct((steps, depth), jnp.float32),
            jax.ShapeDtypeStruct((steps, depth), jnp.float32),
            jax.ShapeDtypeStruct((8, LANES), jnp.float32),
        ],
        compiler_params=params(16),
        cost_estimate=cost(60_000_000, 3_000_000),
        name="tables",
    )(points, slot_waves, early)


def level_weights(scales, me, spare):
    level = jnp.arange(scales.shape[0])[:, None]
    row = jnp.arange(16)[None] % 8
    summed = jnp.where(level >= me, scales[:, None], 0.0)
    weights = jnp.where(row >= spare, summed, (level == me).astype(jnp.float32))
    return jnp.broadcast_to(weights[:, :, None], weights.shape + (LANES,))


def synth_kernel(points_ref, w_ref, r_ref, t_ref, c_ref, s_ref, v_ref, h_ref, g_ref):
    sources, levels = r_ref.shape[:2]
    depth = c_ref.shape[1]
    slots = depth // sources
    fields = v_ref.shape[1]
    pieces = []
    for e in range(sources):
        rows = sum(w_ref[v] * r_ref[e, v].astype(jnp.float32) for v in range(levels))
        pieces.append(rows[:, :slots])
    every = jnp.concatenate(pieces, 1)
    real, imag = every[:8], every[8:]
    for pair in range(g_ref.shape[0] // 16):
        first, second = [], []
        for b in (2 * pair, 2 * pair + 1):
            cosine, sine = c_ref[b : b + 1, :], s_ref[b : b + 1, :]
            first.append(real * cosine - imag * sine)
            second.append(real * sine + imag * cosine)
        to = slice(pair * 16, pair * 16 + 16)
        g_ref[to, :depth] = jnp.concatenate(first, 0).astype(g_ref.dtype)
        g_ref[to, depth:] = jnp.concatenate(second, 0).astype(g_ref.dtype)
    table = t_ref[...].reshape(2 * depth, FINE)
    values = jnp.dot(g_ref[...], table, preferred_element_type=jnp.float32)
    lane = lax.broadcasted_iota(jnp.int32, (8, FINE), 1)
    for b in range(COARSE):
        at = slice(b * FINE, (b + 1) * FINE)
        part = jnp.where(lane + b * FINE < points_ref[0], values[8 * b : 8 * b + 8], 0.0)
        for h in range(2):
            for f in range(fields):
                v_ref[h, f, :, at] = part[h * fields + f : h * fields + f + 1]
            h_ref[h, 0, :, at] = part[2 * fields + h : 2 * fields + h + 1]


def synthesis(points, weights, received, table, cosine, sine, fields):
    depth = cosine.shape[1]
    smem, vmem = pl.BlockSpec(memory_space=pltpu.SMEM), pl.BlockSpec(memory_space=pltpu.VMEM)
    return pl.pallas_call(
        synth_kernel,
        in_specs=[smem] + [vmem] * 5,
        out_specs=[vmem] * 2,
        out_shape=[
            jax.ShapeDtypeStruct((2, fields, 1, PCOL), jnp.float32),
            jax.ShapeDtypeStruct((2, 1, 1, PCOL), jnp.float32),
        ],
        scratch_shapes=[pltpu.VMEM(((COARSE + 1) // 2 * 16, 2 * depth), jnp.bfloat16)],
        compiler_params=params(),
        cost_estimate=cost(1_000_000_000, 3_000_000),
        name="synth",
    )(points, weights, received, table, cosine, sine)


def shards(spectra, legendre, slot_wavenumbers, cycle_points, layer_depth_scaling):
    slots, lats, degrees = legendre.shape
    levels_here, fields = spectra.shape[:2]
    assert levels_here == 1 and cycle_points.shape[0] == 1 and fields == 3
    waves, levels = lax.axis_size("wave"), lax.axis_size("lev")
    columns = fields * 2
    own = lax.dynamic_slice_in_dim(slot_wavenumbers, lax.axis_index("wave") * slots, slots)
    x = spectra.reshape(columns, waves * slots, spectra.shape[4])
    table, cosine, sine, done = tables(cycle_points, slot_wavenumbers[None], legendre)
    scales = lax.all_gather(layer_depth_scaling, "lev", tiled=True)
    weights = level_weights(scales, lax.axis_index("lev"), 2 * fields)
    if spectra.shape[4] == WIDE + REST and waves % 4 == 0 and fields == 3 and slots % GROUP == 0 and lats == 16:
        sent = pack(jnp.swapaxes(x, 1, 2), waves)
        received = lax.all_to_all(sent, "wave", 0, 0, tiled=True)
        ready = (done, weights)
        rows = section(received, legendre, own[:, None], ready, columns, levels)
    else:
        received = lax.all_to_all(x, "wave", split_axis=1, concat_axis=2, tiled=True)
        rows = plain_section(received, legendre, own, levels)
    rows = rows.reshape(waves * levels, 16, LANES)
    rows = lax.all_to_all(rows, ("wave", "lev"), 0, 0, tiled=True)
    rows = rows.reshape(waves, levels, 16, LANES)
    values, height = synthesis(cycle_points, weights, rows, table, cosine, sine, fields)
    return jnp.transpose(values, (0, 2, 1, 3))[:, :, None], height


def solution(mesh):
    in_specs = (P("lev", None, None, None, "wave"), P("wave", None, None), P(), P("wave"), P("lev"))
    out_specs = (P(None, "wave", "lev", None, None), P(None, "wave", "lev", None))
    call = jax.shard_map(shards, mesh=mesh, in_specs=in_specs, out_specs=out_specs, check_vma=False)

    def whole(*arrays):
        values, height = call(*arrays)
        return values, height

    return whole
```

time: 65 us -> 58.5 us (0.900)
  Pallas kernels: 27.4 us -> 10.5 us
  blocking collectives: 3.01 us -> 15.7 us
  starting transfers between devices: 13.6 us -> 8.37 us
  waiting for transfers between devices: 13.8 us -> 18.1 us
  local copies, waits for them, and re-layouts: 4.61 us -> 3.33 us
    pallas_call x4 -> x3, Pallas kernels: 22.5 us -> 7.57 us  [the longest x1 3.37 us: pack(): pl.pallas_call(pack_kernel, in_specs=[pl.BlockSpec(memory_space=pl.ANY)],...]
    all_to_all x0 -> x1, blocking collectives: none -> 13.3 us  [shards(): rows = lax.all_to_all(rows, ('wave', 'lev'), 0, 0, tiled=True)]
    all_to_all x1, waiting for transfers between devices: 5.59 us -> 18.1 us  [shards(): received = lax.all_to_all(sent, 'wave', 0, 0, tiled=True)]
    all_to_all x1 -> x0, waiting for transfers between devices: 8.22 us -> none  [shards(): rows = lax.all_to_all(rows, ('wave', 'lev'), 0, 0, tiled=True)]
    all_to_all x1 -> x0, starting transfers between devices: 5.26 us -> none  [shards(): rows = lax.all_to_all(rows, ('wave', 'lev'), 0, 0, tiled=True)]
    pallas_call x1, Pallas kernels: 4.84 us -> 2.91 us  [section(): pl.pallas_call(functools.partial(section_kernel, copies), in_specs=[pl.Bl...]
    reshape x2 -> x0, local copies, waits for them, and re-layouts: 0.76 us -> none  [the longest x1 0.69 us: shards(): spread = spread.reshape(parts, 1, lats * GROUP)]
    unnamed x11 -> x17, local copies, waits for them, and re-layouts: 3.08 us -> 3.07 us
  transfers between devices with their start and end apart: 2 -> 1, of which waited for: 2 -> 1; matrix products, arithmetic and copies ran while one was open for 4% -> 3% of each run, Pallas kernels for 24% -> 5%
where the time goes in v1:
time: 58.5 us; the launch traced here: 58.2 us
  waiting for transfers between devices  18.1 us (31%)
  blocking collectives  15.7 us (27%)
  Pallas kernels  10.5 us (18%)
  starting transfers between devices  8.37 us (14%)
  local copies, waits for them, and re-layouts  3.33 us (6%)
  between operations  2.04 us (3%)
    all_to_all x1, waiting for transfers between devices, shards(): received = lax.all_to_all(sent, 'wave', 0, 0, tiled=True)  18.1 us
    all_to_all x1, blocking collectives, shards(): rows = lax.all_to_all(rows, ('wave', 'lev'), 0, 0, tiled=True)  13.3 us
    all_to_all x1, starting transfers between devices, shards(): received = lax.all_to_all(sent, 'wave', 0, 0, tiled=True)  8.37 us
    pallas_call x1, Pallas kernels, pack(): pl.pallas_call(pack_kernel, in_specs=[pl.BlockSpec(memory_space=pl.ANY)],...  3.37 us
    unnamed x17, local copies, waits for them, and re-layouts  3.07 us
    pallas_call x1, Pallas kernels, tables(): pl.pallas_call(table_kernel, grid=(depth // LANES,), in_specs=[pl.BlockSp...  3.02 us
    pallas_call x1, Pallas kernels, section(): pl.pallas_call(functools.partial(section_kernel, copies), in_specs=[pl.Bl...  2.91 us
    unnamed x1, blocking collectives  2.44 us
  transfers between devices with their start and end apart: 1, of which 1 were waited for; matrix products, arithmetic and copies ran while one was open for 3% of the time, Pallas kernels for 5%

profile of v1, /device:TPU:0, one launch (start us, length us, event | category | flops | bytes accessed | tf_op | source)
XLA Modules:
  0.0 58.2 jit_solution(14736039850556792740)
XLA Ops:
  0.6 0.0 copy-start
  0.6 3.4 %pack.1 = bf16[16,304,128]{2,1,0:T(8,128)(2,1)} custom-call(bf16[6,80,1280]{2,1,0:T(8,128)(2,1)} %bitcast.13), custom_call_target="tpu_custom_call" | custom-call | bytes 4000000 | tf_op jit(solution)/shard_map/pack/pallas_call | solution.py:78
  4.0 0.0 copy-start.6
  4.0 0.0 copy-start.5
  4.0 8.4 %all-to-all-start = ((bf16[16,304,128]{2,1,0:T(8,128)(2,1)}), bf16[16,304,128]{2,1,0:T(8,128)(2,1)}, u32[]{:S(2)}, u32[]{:S(2)}) async-start(bf16[16,304,128]{2,1,0:T(8,128)(2,1)} %pack.1), calls=%async_computation | async-start | bytes 2490368 | tf_op jit(solution)/shard_map/all_to_all | solution.py:328
  13.1 0.0 copy-done.6
  13.1 0.6 %dynamic-slice = u32[1]{0:T(128)} dynamic-slice(u32[32]{0:T(128)S(1)} %copy-done.6, u32[]{:T(128)S(6)} %add.16), dynamic_slice_sizes={1} | dynamic-slice | bytes 12
  13.7 0.8 %dynamic-update-slice = f32[2]{0:T(128)S(1)} dynamic-update-slice(f32[2]{0:T(128)S(1)} %broadcast.71, f32[1]{0:T(128)S(6)} %copy.11, u32[]{:T(128)} %bitcast) | dynamic-update-slice | bytes 12
  14.4 2.4 %all-reduce = f32[2]{0:T(128)S(1)} all-reduce(f32[2]{0:T(128)S(1)} %dynamic-update-slice), channel_id=1, replica_groups=mesh['wave'=16,'lev'=2] {'lev'}, use_global_device_ids=true, to_apply=%add | all-reduce | flops 2 | bytes 16
  17.5 0.0 copy-done.5
  17.5 0.1 dynamic-slice_bitcast_fusion
  17.6 0.1 copy.7.m_ref
  17.7 0.0 copy-done
  17.7 3.0 %tables.1 = (bf16[2,1280,256]{2,1,0:T(8,128)(2,1)S(1)}, f32[24,1280]{1,0:T(8,128)S(1)}, f32[24,1280]{1,0:T(8,128)S(1)}, f32[8,128]{1,0:T(8,128)S(1)}) custom-call(s32[1]{0:T(128)S(6)} %copy.10.points_ref, s32[1,1280]{1,0:T(1,128)S(1)} %broadcast_in_dim.49.m_ref, bf16[80,16,1280]{2,1,0:T(8,128)(2,1)S(1)} %copy-done), custom_call_target="tpu_custom_call" | custom-call | flops 60000000 | bytes 3000000 | tf_op jit(solution)/shard_map/tables/pallas_call | solution.py:231
  20.8 0.0 copy-start.1
  20.8 1.1 %copy-done.1 = bf16[2,1280,256]{2,1,0:T(8,128)(2,1)} copy-done((bf16[2,1280,256]{2,1,0:T(8,128)(2,1)}, bf16[2,1280,256]{2,1,0:T(8,128)(2,1)S(1)}, u32[]{:S(2)}) %copy-start.1) | copy-done | bytes 1310744
  21.8 0.0 copy-start.3
  21.8 0.6 %copy-done.3 = f32[24,1280]{1,0:T(8,128)} copy-done((f32[24,1280]{1,0:T(8,128)}, f32[24,1280]{1,0:T(8,128)S(1)}, u32[]{:S(2)}) %copy-start.3) | copy-done | bytes 122904
  22.5 0.1 broadcast_select_fusion
  22.6 18.1 %all-to-all-done.r_hbm = bf16[16,304,128]{2,1,0:T(8,128)(2,1)} async-done(((bf16[16,304,128]{2,1,0:T(8,128)(2,1)}), bf16[16,304,128]{2,1,0:T(8,128)(2,1)}, u32[]{:S(2)}, u32[]{:S(2)}) %all-to-all-start) | async-done | bytes 1245216 | tf_op jit(solution)/shard_map/all_to_all | solution.py:328
  40.7 0.1 broadcast_in_dim.47.rest_1_.w_ref
  40.8 0.0 copy-start.2
  40.8 0.0 copy-start.4
  40.8 2.9 %section.1 = bf16[16,2,16,128]{3,2,1,0:T(8,128)(2,1)S(1)} custom-call(bf16[16,304,128]{2,1,0:T(8,128)(2,1)} %all-to-all-done.r_hbm, bf16[80,16,1280]{2,1,0:T(8,128)(2,1)S(1)} %copy-done, s32[80,1]{1,0:T(8,128)S(1)} %copy.7.m_ref, f32[8,128]{1,0:T(8,128)S(1)} %get-tuple-element.8.rest_0_, f32[2,16,128]{2,1,0:T(8,128)S(1)} %broadcast_in_dim.47.rest_1_.w_ref), custom_call_target="tpu_custom_call" | custom-call | flops 10000000000 | bytes 4000000 | tf_op jit(solution)/shard_map/section/pallas_call | solution.py:158
  43.7 13.3 %all_to_all.10 = bf16[32,16,128]{2,1,0:T(8,128)(2,1)S(1)} all-to-all(bf16[32,16,128]{2,1,0:T(8,128)(2,1)S(1)} %bitcast.12), channel_id=1, replica_groups=mesh['wave'=16,'lev'=2] {'wave','lev'}, dimensions={0} | all-to-all | bytes 262144 | tf_op jit(solution)/shard_map/all_to_all | solution.py:335
  57.0 0.0 copy-done.2
  57.0 0.0 copy-done.4
  57.0 1.2 %synth.1 = (f32[2,3,1,5376]{3,2,1,0:T(1,128)}, f32[2,1,1,5376]{3,2,1,0:T(1,128)}) custom-call(s32[1]{0:T(128)S(6)} %copy.10.points_ref, f32[2,16,128]{2,1,0:T(8,128)S(1)} %broadcast_in_dim.47.rest_1_.w_ref, bf16[16,2,16,128]{3,2,1,0:T(8,128)(2,1)S(1)} %bitcast.11, bf16[2,1280,256]{2,1,0:T(8,128)(2,1)S(1)} %copy-done.2, ...), custom_call_target="tpu_custom_call" | custom-call | flops 1000000000 | bytes 3000000 | tf_op jit(solution)/shard_map/synth/pallas_call | solution.py:300
  (5 shorter events, 0.0 us)
Async XLA Ops:
  0.6 17.1 %copy-start = (bf16[80,16,1280]{2,1,0:T(8,128)(2,1)S(1)}, bf16[80,16,1280]{2,1,0:T(8,128)(2,1)}, u32[]{:S(2)}) copy-start(bf16[80,16,1280]{2,1,0:T(8,128)(2,1)} %x_ref.1) | copy-start | bytes 9830404
  4.0 9.1 %copy-start.6 = (u32[32]{0:T(128)S(1)}, u32[32]{0:T(128)}, u32[]{:S(2)}) copy-start(u32[32]{0:T(128)} %constant.38) | copy-start | bytes 388
  4.0 13.5 %copy-start.5 = (s32[1280]{0:T(1024)S(1)}, s32[1280]{0:T(1024)}, u32[]{:S(2)}) copy-start(s32[1280]{0:T(1024)} %param.7) | copy-start | bytes 15364
  4.0 36.7 %all-to-all-start = ((bf16[16,304,128]{2,1,0:T(8,128)(2,1)}), bf16[16,304,128]{2,1,0:T(8,128)(2,1)}, u32[]{:S(2)}, u32[]{:S(2)}) async-start(bf16[16,304,128]{2,1,0:T(8,128)(2,1)} %pack.1), calls=%async_computation | async-start | bytes 2490368 | tf_op jit(solution)/shard_map/all_to_all | solution.py:328
  20.8 1.1 %copy-start.1 = (bf16[2,1280,256]{2,1,0:T(8,128)(2,1)}, bf16[2,1280,256]{2,1,0:T(8,128)(2,1)S(1)}, u32[]{:S(2)}) copy-start(bf16[2,1280,256]{2,1,0:T(8,128)(2,1)S(1)} %get-tuple-element.9.t_ref) | copy-start | bytes 3932164
  21.8 0.6 %copy-start.3 = (f32[24,1280]{1,0:T(8,128)}, f32[24,1280]{1,0:T(8,128)S(1)}, u32[]{:S(2)}) copy-start(f32[24,1280]{1,0:T(8,128)S(1)} %get-tuple-element.11.s_ref) | copy-start | bytes 368644
  40.8 16.2 %copy-start.2 = (bf16[2,1280,256]{2,1,0:T(8,128)(2,1)S(1)}, bf16[2,1280,256]{2,1,0:T(8,128)(2,1)}, u32[]{:S(2)}) copy-start(bf16[2,1280,256]{2,1,0:T(8,128)(2,1)} %copy-done.1) | copy-start | bytes 3932164
  40.8 16.2 %copy-start.4 = (f32[24,1280]{1,0:T(8,128)S(1)}, f32[24,1280]{1,0:T(8,128)}, u32[]{:S(2)}) copy-start(f32[24,1280]{1,0:T(8,128)} %copy-done.3) | copy-start | bytes 368644

commit v2 on v1

--- a/solution.py
+++ b/solution.py
@@ -25,44 +25,39 @@
     return pltpu.CompilerParams(vmem_limit_bytes=size * 1024 * 1024)
 
 
-def block_rows(columns, slots):
-    groups = columns * slots // GROUP
-    return (groups // 2 + -(-groups // 8)) * GROUP
+def rest_place(c, g):
+    return (g, c * REST) if g < 4 else (c // 2, (6 + c % 2) * REST)
 
 
 def pack_kernel(x_hbm, o_hbm, x_ref, o_ref, in_sems, out_sems):
     columns, _, rows = x_ref.shape
     targets = o_ref.shape[0]
     slots = rows // targets
-    parts = slots // GROUP
-    groups = columns * parts
+    fields = columns // 2
     loads, stores = [], []
-    for i in range(2):
-        some = pl.ds(i * columns // 2, columns // 2)
-        loads.append(pltpu.make_async_copy(x_hbm.at[some], x_ref.at[some], in_sems.at[i]))
-        loads[i].start()
-    turned = []
-    for c in range(columns):
-        if c % (columns // 2) == 0:
-            loads[c // (columns // 2)].wait()
-        turned.append(jnp.transpose(x_ref[c]))
+    for f in range(fields):
+        some = pl.ds(2 * f, 2)
+        loads.append(pltpu.make_async_copy(x_hbm.at[some], x_ref.at[some], in_sems.at[f]))
+        loads[f].start()
+    wide = []
+    for f in range(fields):
+        loads[f].wait()
+        both = jnp.concatenate([x_ref[2 * f, :WIDE, :], x_ref[2 * f + 1, :WIDE, :]], 0)
+        wide.append(jnp.transpose(both))
+    last = [x_ref[c, WIDE:, :] for c in range(columns)]
+    rest = jnp.transpose(jnp.concatenate(last + last[:2], 0))
     chunk = targets // 4
     for t in range(targets):
         base = t * slots
-        for g in range(parts):
-            s = slice(base + g * GROUP, base + (g + 1) * GROUP)
-            for f in range(columns // 2):
-                at = (g * columns // 2 + f) * GROUP
-                real, imag = turned[2 * f][s, :WIDE], turned[2 * f + 1][s, :WIDE]
-                o_ref[t, at : at + GROUP, :] = jnp.concatenate([real, imag], 1)
-        start = columns // 2 * slots
-        for r in range(-(-groups // 8)):
-            pieces = []
-            for k in range(8):
-                q = min(8 * r + k, groups - 1)
-                s = base + q // columns * GROUP
-                pieces.append(turned[q % columns][s : s + GROUP, WIDE:])
-            o_ref[t, start + r * GROUP : start + (r + 1) * GROUP, :] = jnp.concatenate(pieces, 1)
+        for f in range(fields):
+            o_ref[t, f * slots : (f + 1) * slots, :] = wide[f][base : base + slots]
+        groups = [rest[base + g * GROUP : base + (g + 1) * GROUP] for g in range(5)]
+        for g in range(4):
+            at = fields * slots + g * GROUP
+            tile = groups[g]
+            if g < fields:
+                tile = jnp.concatenate([tile[:, : 6 * REST], groups[4][:, 2 * g * REST : 2 * (g + 1) * REST]], 1)
+            o_ref[t, at : at + GROUP, :] = tile
         if (t + 1) % chunk == 0:
             i = t // chunk
             some = pl.ds(i * chunk, chunk)
@@ -74,7 +69,7 @@
 
 def pack(x, targets):
     columns, degrees, rows = x.shape
-    out = (targets, block_rows(columns, rows // targets), LANES)
+    out = (targets, columns // 2 * (rows // targets) + 4 * GROUP, LANES)
     return pl.pallas_call(
         pack_kernel,
         in_specs=[pl.BlockSpec(memory_space=pl.ANY)],
@@ -83,7 +78,7 @@
         scratch_shapes=[
             pltpu.VMEM(x.shape, x.dtype),
             pltpu.VMEM(out, x.dtype),
-            pltpu.SemaphoreType.DMA((2,)),
+            pltpu.SemaphoreType.DMA((columns // 2,)),
             pltpu.SemaphoreType.DMA((4,)),
         ],
         compiler_params=params(56),
@@ -101,25 +96,31 @@
     columns = s_ref.shape[1] // (2 * GROUP)
     fields = columns // 2
     half = columns * GROUP
-    start = columns // 2 * slots
     arrive = pltpu.make_async_copy(r_hbm, r_ref, sem)
     arrive.start()
     row = lax.broadcasted_iota(jnp.int32, (2 * half, width), 0)
     lane = lax.broadcasted_iota(jnp.int32, (2 * half, width), 1)
     same = (row % GROUP == lane // lats).reshape(2 * columns, GROUP, width)
     degree = lax.broadcasted_iota(jnp.int32, (GROUP, degrees), 1)
-    arrive.wait()
+    source = lax.broadcasted_iota(jnp.int32, (width, width), 0)
+    target = lax.broadcasted_iota(jnp.int32, (width, width), 1)
+    move = (target == source % lats * GROUP + source // lats).astype(jnp.float32).astype(s_ref.dtype)
+    masks = []
     for g in range(parts):
         wave = m_ref[g * GROUP : (g + 1) * GROUP, :]
         live = degree >= wave
         sign = (1 - 2 * ((degree + wave) % 2)).astype(jnp.float32)
         north = jnp.where(live, 1.0, 0.0).astype(s_ref.dtype)
         south = jnp.where(live, sign, 0.0).astype(s_ref.dtype)
+        masks.append((north, south))
+    arrive.wait()
+    for g in range(parts):
+        north, south = masks[g]
         for c in range(columns):
-            at = (g * columns // 2 + c // 2) * GROUP
+            at = c // 2 * slots + g * GROUP
             lo = c % 2 * WIDE
-            q = g * columns + c
-            rest_at, rest_lo = start + q // 8 * GROUP, q % 8 * REST
+            tile, rest_lo = rest_place(c, g)
+            rest_at = fields * slots + tile * GROUP
             pieces = []
             for e in range(sources):
                 pieces.append(r_ref[e, at : at + GROUP, lo : lo + WIDE])
@@ -139,9 +140,6 @@
             f_ref[at : at + 2 * fields, :] = found[first : first + 2 * fields]
             f_ref[at + 2 * fields : at + 2 * fields + 1, :] = found[first : first + 1]
             f_ref[at + 2 * fields + 1 : at + 8, :] = found[first + fields : first + fields + 1]
-    source = lax.broadcasted_iota(jnp.int32, (width, width), 0)
-    target = lax.broadcasted_iota(jnp.int32, (width, width), 1)
-    move = (target == source % lats * GROUP + source // lats).astype(jnp.float32).astype(s_ref.dtype)
     moved = jnp.dot(f_ref[...].astype(s_ref.dtype), move, preferred_element_type=jnp.float32)
     blank = jnp.zeros((16, LANES - slots), jnp.float32)
     for l in range(lats):
@@ -323,7 +321,7 @@
     table, cosine, sine, done = tables(cycle_points, slot_wavenumbers[None], legendre)
     scales = lax.all_gather(layer_depth_scaling, "lev", tiled=True)
     weights = level_weights(scales, lax.axis_index("lev"), 2 * fields)
-    if spectra.shape[4] == WIDE + REST and waves % 4 == 0 and fields == 3 and slots % GROUP == 0 and lats == 16:
+    if spectra.shape[4] == WIDE + REST and waves % 4 == 0 and fields == 3 and slots == 5 * GROUP and lats == 16:
         sent = pack(jnp.swapaxes(x, 1, 2), waves)
         received = lax.all_to_all(sent, "wave", 0, 0, tiled=True)
         ready = (done, weights)

time: 58.5 us -> 57.9 us (0.990)
  Pallas kernels: 10.5 us -> 9.86 us
where the time goes in v2:
time: 57.9 us; the launch traced here: 57.6 us
  waiting for transfers between devices  18.1 us (31%)
  blocking collectives  15.7 us (27%)
  Pallas kernels  9.86 us (17%)
  starting transfers between devices  8.37 us (14%)
  local copies, waits for them, and re-layouts  3.33 us (6%)
  between operations  2.04 us (4%)
    all_to_all x1, waiting for transfers between devices, shards(): received = lax.all_to_all(sent, 'wave', 0, 0, tiled=True)  18.1 us
    all_to_all x1, blocking collectives, shards(): rows = lax.all_to_all(rows, ('wave', 'lev'), 0, 0, tiled=True)  13.3 us
    all_to_all x1, starting transfers between devices, shards(): received = lax.all_to_all(sent, 'wave', 0, 0, tiled=True)  8.37 us
    unnamed x17, local copies, waits for them, and re-layouts  3.07 us
    pallas_call x1, Pallas kernels, tables(): pl.pallas_call(table_kernel, grid=(depth // LANES,), in_specs=[pl.BlockSp...  3.02 us
    pallas_call x1, Pallas kernels, section(): pl.pallas_call(functools.partial(section_kernel, copies), in_specs=[pl.Bl...  2.86 us
    pallas_call x1, Pallas kernels, pack(): pl.pallas_call(pack_kernel, in_specs=[pl.BlockSpec(memory_space=pl.ANY)],...  2.8 us
    unnamed x1, blocking collectives  2.44 us
  transfers between devices with their start and end apart: 1, of which 1 were waited for; matrix products, arithmetic and copies ran while one was open for 3% of the time, Pallas kernels for 5%

profile of v2, /device:TPU:0, one launch (start us, length us, event | category | flops | bytes accessed | tf_op | source)
XLA Modules:
  0.0 57.6 jit_solution(10054540156486738176)
XLA Ops:
  0.6 0.0 copy-start
  0.6 2.8 %pack.1 = bf16[16,304,128]{2,1,0:T(8,128)(2,1)} custom-call(bf16[6,80,1280]{2,1,0:T(8,128)(2,1)} %bitcast.13), custom_call_target="tpu_custom_call" | custom-call | bytes 4000000 | tf_op jit(solution)/shard_map/pack/pallas_call | solution.py:73
  3.4 0.0 copy-start.6
  3.5 0.0 copy-start.5
  3.5 8.4 %all-to-all-start = ((bf16[16,304,128]{2,1,0:T(8,128)(2,1)}), bf16[16,304,128]{2,1,0:T(8,128)(2,1)}, u32[]{:S(2)}, u32[]{:S(2)}) async-start(bf16[16,304,128]{2,1,0:T(8,128)(2,1)} %pack.1), calls=%async_computation | async-start | bytes 2490368 | tf_op jit(solution)/shard_map/all_to_all | solution.py:326
  12.5 0.0 copy-done.6
  12.5 0.6 %dynamic-slice = u32[1]{0:T(128)} dynamic-slice(u32[32]{0:T(128)S(1)} %copy-done.6, u32[]{:T(128)S(6)} %add.16), dynamic_slice_sizes={1} | dynamic-slice | bytes 12
  13.1 0.8 %dynamic-update-slice = f32[2]{0:T(128)S(1)} dynamic-update-slice(f32[2]{0:T(128)S(1)} %broadcast.71, f32[1]{0:T(128)S(6)} %copy.11, u32[]{:T(128)} %bitcast) | dynamic-update-slice | bytes 12
  13.9 2.4 %all-reduce = f32[2]{0:T(128)S(1)} all-reduce(f32[2]{0:T(128)S(1)} %dynamic-update-slice), channel_id=1, replica_groups=mesh['wave'=16,'lev'=2] {'lev'}, use_global_device_ids=true, to_apply=%add | all-reduce | flops 2 | bytes 16
  16.9 0.0 copy-done.5
  17.0 0.1 dynamic-slice_bitcast_fusion
  17.1 0.1 copy.7.m_ref
  17.2 0.0 copy-done
  17.2 3.0 %tables.1 = (bf16[2,1280,256]{2,1,0:T(8,128)(2,1)S(1)}, f32[24,1280]{1,0:T(8,128)S(1)}, f32[24,1280]{1,0:T(8,128)S(1)}, f32[8,128]{1,0:T(8,128)S(1)}) custom-call(s32[1]{0:T(128)S(6)} %copy.10.points_ref, s32[1,1280]{1,0:T(1,128)S(1)} %broadcast_in_dim.49.m_ref, bf16[80,16,1280]{2,1,0:T(8,128)(2,1)S(1)} %copy-done), custom_call_target="tpu_custom_call" | custom-call | flops 60000000 | bytes 3000000 | tf_op jit(solution)/shard_map/tables/pallas_call | solution.py:229
  20.2 0.0 copy-start.1
  20.2 1.1 %copy-done.1 = bf16[2,1280,256]{2,1,0:T(8,128)(2,1)} copy-done((bf16[2,1280,256]{2,1,0:T(8,128)(2,1)}, bf16[2,1280,256]{2,1,0:T(8,128)(2,1)S(1)}, u32[]{:S(2)}) %copy-start.1) | copy-done | bytes 1310744
  21.3 0.0 copy-start.3
  21.3 0.6 %copy-done.3 = f32[24,1280]{1,0:T(8,128)} copy-done((f32[24,1280]{1,0:T(8,128)}, f32[24,1280]{1,0:T(8,128)S(1)}, u32[]{:S(2)}) %copy-start.3) | copy-done | bytes 122904
  21.9 0.1 broadcast_select_fusion
  22.0 18.1 %all-to-all-done.r_hbm = bf16[16,304,128]{2,1,0:T(8,128)(2,1)} async-done(((bf16[16,304,128]{2,1,0:T(8,128)(2,1)}), bf16[16,304,128]{2,1,0:T(8,128)(2,1)}, u32[]{:S(2)}, u32[]{:S(2)}) %all-to-all-start) | async-done | bytes 1245216 | tf_op jit(solution)/shard_map/all_to_all | solution.py:326
  40.1 0.1 broadcast_in_dim.47.rest_1_.w_ref
  40.2 0.0 copy-start.2
  40.2 0.0 copy-start.4
  40.2 2.9 %section.1 = bf16[16,2,16,128]{3,2,1,0:T(8,128)(2,1)S(1)} custom-call(bf16[16,304,128]{2,1,0:T(8,128)(2,1)} %all-to-all-done.r_hbm, bf16[80,16,1280]{2,1,0:T(8,128)(2,1)S(1)} %copy-done, s32[80,1]{1,0:T(8,128)S(1)} %copy.7.m_ref, f32[8,128]{1,0:T(8,128)S(1)} %get-tuple-element.8.rest_0_, f32[2,16,128]{2,1,0:T(8,128)S(1)} %broadcast_in_dim.47.rest_1_.w_ref), custom_call_target="tpu_custom_call" | custom-call | flops 10000000000 | bytes 4000000 | tf_op jit(solution)/shard_map/section/pallas_call | solution.py:156
  43.1 13.3 %all_to_all.10 = bf16[32,16,128]{2,1,0:T(8,128)(2,1)S(1)} all-to-all(bf16[32,16,128]{2,1,0:T(8,128)(2,1)S(1)} %bitcast.12), channel_id=1, replica_groups=mesh['wave'=16,'lev'=2] {'wave','lev'}, dimensions={0} | all-to-all | bytes 262144 | tf_op jit(solution)/shard_map/all_to_all | solution.py:333
  56.4 0.0 copy-done.2
  56.4 0.0 copy-done.4
  56.4 1.2 %synth.1 = (f32[2,3,1,5376]{3,2,1,0:T(1,128)}, f32[2,1,1,5376]{3,2,1,0:T(1,128)}) custom-call(s32[1]{0:T(128)S(6)} %copy.10.points_ref, f32[2,16,128]{2,1,0:T(8,128)S(1)} %broadcast_in_dim.47.rest_1_.w_ref, bf16[16,2,16,128]{3,2,1,0:T(8,128)(2,1)S(1)} %bitcast.11, bf16[2,1280,256]{2,1,0:T(8,128)(2,1)S(1)} %copy-done.2, ...), custom_call_target="tpu_custom_call" | custom-call | flops 1000000000 | bytes 3000000 | tf_op jit(solution)/shard_map/synth/pallas_call | solution.py:298
  (5 shorter events, 0.0 us)
Async XLA Ops:
  0.6 16.5 %copy-start = (bf16[80,16,1280]{2,1,0:T(8,128)(2,1)S(1)}, bf16[80,16,1280]{2,1,0:T(8,128)(2,1)}, u32[]{:S(2)}) copy-start(bf16[80,16,1280]{2,1,0:T(8,128)(2,1)} %x_ref.1) | copy-start | bytes 9830404
  3.4 9.1 %copy-start.6 = (u32[32]{0:T(128)S(1)}, u32[32]{0:T(128)}, u32[]{:S(2)}) copy-start(u32[32]{0:T(128)} %constant.38) | copy-start | bytes 388
  3.5 13.5 %copy-start.5 = (s32[1280]{0:T(1024)S(1)}, s32[1280]{0:T(1024)}, u32[]{:S(2)}) copy-start(s32[1280]{0:T(1024)} %param.7) | copy-start | bytes 15364
  3.5 36.7 %all-to-all-start = ((bf16[16,304,128]{2,1,0:T(8,128)(2,1)}), bf16[16,304,128]{2,1,0:T(8,128)(2,1)}, u32[]{:S(2)}, u32[]{:S(2)}) async-start(bf16[16,304,128]{2,1,0:T(8,128)(2,1)} %pack.1), calls=%async_computation | async-start | bytes 2490368 | tf_op jit(solution)/shard_map/all_to_all | solution.py:326
  20.2 1.1 %copy-start.1 = (bf16[2,1280,256]{2,1,0:T(8,128)(2,1)}, bf16[2,1280,256]{2,1,0:T(8,128)(2,1)S(1)}, u32[]{:S(2)}) copy-start(bf16[2,1280,256]{2,1,0:T(8,128)(2,1)S(1)} %get-tuple-element.9.t_ref) | copy-start | bytes 3932164
  21.3 0.6 %copy-start.3 = (f32[24,1280]{1,0:T(8,128)}, f32[24,1280]{1,0:T(8,128)S(1)}, u32[]{:S(2)}) copy-start(f32[24,1280]{1,0:T(8,128)S(1)} %get-tuple-element.11.s_ref) | copy-start | bytes 368644
  40.2 16.2 %copy-start.2 = (bf16[2,1280,256]{2,1,0:T(8,128)(2,1)S(1)}, bf16[2,1280,256]{2,1,0:T(8,128)(2,1)}, u32[]{:S(2)}) copy-start(bf16[2,1280,256]{2,1,0:T(8,128)(2,1)} %copy-done.1) | copy-start | bytes 3932164
  40.2 16.2 %copy-start.4 = (f32[24,1280]{1,0:T(8,128)S(1)}, f32[24,1280]{1,0:T(8,128)}, u32[]{:S(2)}) copy-start(f32[24,1280]{1,0:T(8,128)} %copy-done.3) | copy-start | bytes 368644

commit v3 on v2

--- a/solution.py
+++ b/solution.py
@@ -23,6 +23,11 @@
 
 def params(size=16):
     return pltpu.CompilerParams(vmem_limit_bytes=size * 1024 * 1024)
+
+
+def exchange_order(devices):
+    bits = (devices - 1).bit_length()
+    return sorted(range(devices), key=lambda i: int(format(i, "0" + str(bits) + "b")[::-1], 2))
 
 
 def rest_place(c, g):
@@ -47,8 +52,8 @@
     last = [x_ref[c, WIDE:, :] for c in range(columns)]
     rest = jnp.transpose(jnp.concatenate(last + last[:2], 0))
     chunk = targets // 4
-    for t in range(targets):
-        base = t * slots
+    for t, target in enumerate(exchange_order(targets)):
+        base = target * slots
         for f in range(fields):
             o_ref[t, f * slots : (f + 1) * slots, :] = wide[f][base : base + slots]
         groups = [rest[base + g * GROUP : base + (g + 1) * GROUP] for g in range(5)]
@@ -96,6 +101,8 @@
     columns = s_ref.shape[1] // (2 * GROUP)
     fields = columns // 2
     half = columns * GROUP
+    order = exchange_order(sources)
+    places = [order.index(e) for e in range(sources)]
     arrive = pltpu.make_async_copy(r_hbm, r_ref, sem)
     arrive.start()
     row = lax.broadcasted_iota(jnp.int32, (2 * half, width), 0)
@@ -122,7 +129,7 @@
             tile, rest_lo = rest_place(c, g)
             rest_at = fields * slots + tile * GROUP
             pieces = []
-            for e in range(sources):
+            for e in places:
                 pieces.append(r_ref[e, at : at + GROUP, lo : lo + WIDE])
                 pieces.append(r_ref[e, rest_at : rest_at + GROUP, rest_lo : rest_lo + REST])
             tile = jnp.concatenate(pieces, 1)
@@ -323,7 +330,8 @@
     weights = level_weights(scales, lax.axis_index("lev"), 2 * fields)
     if spectra.shape[4] == WIDE + REST and waves % 4 == 0 and fields == 3 and slots == 5 * GROUP and lats == 16:
         sent = pack(jnp.swapaxes(x, 1, 2), waves)
-        received = lax.all_to_all(sent, "wave", 0, 0, tiled=True)
+        order = [exchange_order(waves)]
+        received = lax.all_to_all(sent, "wave", 0, 0, axis_index_groups=order, tiled=True)
         ready = (done, weights)
         rows = section(received, legendre, own[:, None], ready, columns, levels)
     else:

time: 57.9 us -> 57.1 us (0.986)
  blocking collectives: 15.7 us -> 13.3 us
  waiting for transfers between devices: 18.1 us -> 19.8 us
    all_to_all x1, blocking collectives: 13.3 us -> 10.9 us  [shards(): rows = lax.all_to_all(rows, ('wave', 'lev'), 0, 0, tiled=True)]
    all_to_all x1, waiting for transfers between devices: 18.1 us -> 19.8 us  [shards(): lax.all_to_all(sent, 'wave', 0, 0, axis_index_groups=order, tiled=True)]
where the time goes in v3:
time: 57.1 us; the launch traced here: 56.8 us
  waiting for transfers between devices  19.8 us (35%)
  blocking collectives  13.3 us (23%)
  Pallas kernels  9.89 us (17%)
  starting transfers between devices  8.37 us (15%)
  local copies, waits for them, and re-layouts  3.33 us (6%)
  between operations  2.04 us (4%)
    all_to_all x1, waiting for transfers between devices, shards(): lax.all_to_all(sent, 'wave', 0, 0, axis_index_groups=order, tiled=True)  19.8 us
    all_to_all x1, blocking collectives, shards(): rows = lax.all_to_all(rows, ('wave', 'lev'), 0, 0, tiled=True)  10.9 us
    all_to_all x1, starting transfers between devices, shards(): lax.all_to_all(sent, 'wave', 0, 0, axis_index_groups=order, tiled=True)  8.37 us
    unnamed x17, local copies, waits for them, and re-layouts  3.07 us
    pallas_call x1, Pallas kernels, tables(): pl.pallas_call(table_kernel, grid=(depth // LANES,), in_specs=[pl.BlockSp...  3.02 us
    pallas_call x1, Pallas kernels, section(): pl.pallas_call(functools.partial(section_kernel, copies), in_specs=[pl.Bl...  2.86 us
    pallas_call x1, Pallas kernels, pack(): pl.pallas_call(pack_kernel, in_specs=[pl.BlockSpec(memory_space=pl.ANY)],...  2.83 us
    unnamed x1, blocking collectives  2.44 us
  transfers between devices with their start and end apart: 1, of which 1 were waited for; matrix products, arithmetic and copies ran while one was open for 3% of the time, Pallas kernels for 5%

profile of v3, /device:TPU:0, one launch (start us, length us, event | category | flops | bytes accessed | tf_op | source)
XLA Modules:
  0.0 56.8 jit_solution(10627043662755809696)
XLA Ops:
  0.6 0.0 copy-start
  0.6 2.8 %pack.1 = bf16[16,304,128]{2,1,0:T(8,128)(2,1)} custom-call(bf16[6,80,1280]{2,1,0:T(8,128)(2,1)} %bitcast.13), custom_call_target="tpu_custom_call" | custom-call | bytes 4000000 | tf_op jit(solution)/shard_map/pack/pallas_call | solution.py:78
  3.5 0.0 copy-start.6
  3.5 0.0 copy-start.5
  3.5 8.4 %all-to-all-start = ((bf16[16,304,128]{2,1,0:T(8,128)(2,1)}), bf16[16,304,128]{2,1,0:T(8,128)(2,1)}, u32[]{:S(2)}, u32[]{:S(2)}) async-start(bf16[16,304,128]{2,1,0:T(8,128)(2,1)} %pack.1), calls=%async_computation | async-start | bytes 2490368 | tf_op jit(solution)/shard_map/all_to_all | solution.py:334
  12.5 0.0 copy-done.6
  12.5 0.6 %dynamic-slice = u32[1]{0:T(128)} dynamic-slice(u32[32]{0:T(128)S(1)} %copy-done.6, u32[]{:T(128)S(6)} %add.16), dynamic_slice_sizes={1} | dynamic-slice | bytes 12
  13.1 0.8 %dynamic-update-slice = f32[2]{0:T(128)S(1)} dynamic-update-slice(f32[2]{0:T(128)S(1)} %broadcast.71, f32[1]{0:T(128)S(6)} %copy.11, u32[]{:T(128)} %bitcast) | dynamic-update-slice | bytes 12
  13.9 2.4 %all-reduce = f32[2]{0:T(128)S(1)} all-reduce(f32[2]{0:T(128)S(1)} %dynamic-update-slice), channel_id=1, replica_groups=mesh['wave'=16,'lev'=2] {'lev'}, use_global_device_ids=true, to_apply=%add | all-reduce | flops 2 | bytes 16
  17.0 0.0 copy-done.5
  17.0 0.1 dynamic-slice_bitcast_fusion
  17.1 0.1 copy.7.m_ref
  17.2 0.0 copy-done
  17.2 3.0 %tables.1 = (bf16[2,1280,256]{2,1,0:T(8,128)(2,1)S(1)}, f32[24,1280]{1,0:T(8,128)S(1)}, f32[24,1280]{1,0:T(8,128)S(1)}, f32[8,128]{1,0:T(8,128)S(1)}) custom-call(s32[1]{0:T(128)S(6)} %copy.10.points_ref, s32[1,1280]{1,0:T(1,128)S(1)} %broadcast_in_dim.49.m_ref, bf16[80,16,1280]{2,1,0:T(8,128)(2,1)S(1)} %copy-done), custom_call_target="tpu_custom_call" | custom-call | flops 60000000 | bytes 3000000 | tf_op jit(solution)/shard_map/tables/pallas_call | solution.py:236
  20.2 0.0 copy-start.1
  20.2 1.1 %copy-done.1 = bf16[2,1280,256]{2,1,0:T(8,128)(2,1)} copy-done((bf16[2,1280,256]{2,1,0:T(8,128)(2,1)}, bf16[2,1280,256]{2,1,0:T(8,128)(2,1)S(1)}, u32[]{:S(2)}) %copy-start.1) | copy-done | bytes 1310744
  21.3 0.0 copy-start.3
  21.3 0.6 %copy-done.3 = f32[24,1280]{1,0:T(8,128)} copy-done((f32[24,1280]{1,0:T(8,128)}, f32[24,1280]{1,0:T(8,128)S(1)}, u32[]{:S(2)}) %copy-start.3) | copy-done | bytes 122904
  22.0 0.1 broadcast_select_fusion
  22.0 19.8 %all-to-all-done.r_hbm = bf16[16,304,128]{2,1,0:T(8,128)(2,1)} async-done(((bf16[16,304,128]{2,1,0:T(8,128)(2,1)}), bf16[16,304,128]{2,1,0:T(8,128)(2,1)}, u32[]{:S(2)}, u32[]{:S(2)}) %all-to-all-start) | async-done | bytes 1245216 | tf_op jit(solution)/shard_map/all_to_all | solution.py:334
  41.8 0.1 broadcast_in_dim.47.rest_1_.w_ref
  41.9 0.0 copy-start.2
  41.9 0.0 copy-start.4
  41.9 2.9 %section.1 = bf16[16,2,16,128]{3,2,1,0:T(8,128)(2,1)S(1)} custom-call(bf16[16,304,128]{2,1,0:T(8,128)(2,1)} %all-to-all-done.r_hbm, bf16[80,16,1280]{2,1,0:T(8,128)(2,1)S(1)} %copy-done, s32[80,1]{1,0:T(8,128)S(1)} %copy.7.m_ref, f32[8,128]{1,0:T(8,128)S(1)} %get-tuple-element.8.rest_0_, f32[2,16,128]{2,1,0:T(8,128)S(1)} %broadcast_in_dim.47.rest_1_.w_ref), custom_call_target="tpu_custom_call" | custom-call | flops 10000000000 | bytes 4000000 | tf_op jit(solution)/shard_map/section/pallas_call | solution.py:163
  44.8 10.9 %all_to_all.10 = bf16[32,16,128]{2,1,0:T(8,128)(2,1)S(1)} all-to-all(bf16[32,16,128]{2,1,0:T(8,128)(2,1)S(1)} %bitcast.12), channel_id=1, replica_groups=mesh['wave'=16,'lev'=2] {'wave','lev'}, dimensions={0} | all-to-all | bytes 262144 | tf_op jit(solution)/shard_map/all_to_all | solution.py:341
  55.6 0.0 copy-done.2
  55.6 0.0 copy-done.4
  55.6 1.2 %synth.1 = (f32[2,3,1,5376]{3,2,1,0:T(1,128)}, f32[2,1,1,5376]{3,2,1,0:T(1,128)}) custom-call(s32[1]{0:T(128)S(6)} %copy.10.points_ref, f32[2,16,128]{2,1,0:T(8,128)S(1)} %broadcast_in_dim.47.rest_1_.w_ref, bf16[16,2,16,128]{3,2,1,0:T(8,128)(2,1)S(1)} %bitcast.11, bf16[2,1280,256]{2,1,0:T(8,128)(2,1)S(1)} %copy-done.2, ...), custom_call_target="tpu_custom_call" | custom-call | flops 1000000000 | bytes 3000000 | tf_op jit(solution)/shard_map/synth/pallas_call | solution.py:305
  (5 shorter events, 0.0 us)
Async XLA Ops:
  0.6 16.6 %copy-start = (bf16[80,16,1280]{2,1,0:T(8,128)(2,1)S(1)}, bf16[80,16,1280]{2,1,0:T(8,128)(2,1)}, u32[]{:S(2)}) copy-start(bf16[80,16,1280]{2,1,0:T(8,128)(2,1)} %x_ref.1) | copy-start | bytes 9830404
  3.5 9.1 %copy-start.6 = (u32[32]{0:T(128)S(1)}, u32[32]{0:T(128)}, u32[]{:S(2)}) copy-start(u32[32]{0:T(128)} %constant.38) | copy-start | bytes 388
  3.5 13.5 %copy-start.5 = (s32[1280]{0:T(1024)S(1)}, s32[1280]{0:T(1024)}, u32[]{:S(2)}) copy-start(s32[1280]{0:T(1024)} %param.7) | copy-start | bytes 15364
  3.5 38.3 %all-to-all-start = ((bf16[16,304,128]{2,1,0:T(8,128)(2,1)}), bf16[16,304,128]{2,1,0:T(8,128)(2,1)}, u32[]{:S(2)}, u32[]{:S(2)}) async-start(bf16[16,304,128]{2,1,0:T(8,128)(2,1)} %pack.1), calls=%async_computation | async-start | bytes 2490368 | tf_op jit(solution)/shard_map/all_to_all | solution.py:334
  20.2 1.1 %copy-start.1 = (bf16[2,1280,256]{2,1,0:T(8,128)(2,1)}, bf16[2,1280,256]{2,1,0:T(8,128)(2,1)S(1)}, u32[]{:S(2)}) copy-start(bf16[2,1280,256]{2,1,0:T(8,128)(2,1)S(1)} %get-tuple-element.9.t_ref) | copy-start | bytes 3932164
  21.3 0.6 %copy-start.3 = (f32[24,1280]{1,0:T(8,128)}, f32[24,1280]{1,0:T(8,128)S(1)}, u32[]{:S(2)}) copy-start(f32[24,1280]{1,0:T(8,128)S(1)} %get-tuple-element.11.s_ref) | copy-start | bytes 368644
  41.9 13.8 %copy-start.2 = (bf16[2,1280,256]{2,1,0:T(8,128)(2,1)S(1)}, bf16[2,1280,256]{2,1,0:T(8,128)(2,1)}, u32[]{:S(2)}) copy-start(bf16[2,1280,256]{2,1,0:T(8,128)(2,1)} %copy-done.1) | copy-start | bytes 3932164
  41.9 13.8 %copy-start.4 = (f32[24,1280]{1,0:T(8,128)S(1)}, f32[24,1280]{1,0:T(8,128)}, u32[]{:S(2)}) copy-start(f32[24,1280]{1,0:T(8,128)} %copy-done.3) | copy-start | bytes 368644

commit v4 on v3

--- a/solution.py
+++ b/solution.py
@@ -26,8 +26,9 @@
 
 
 def exchange_order(devices):
-    bits = (devices - 1).bit_length()
-    return sorted(range(devices), key=lambda i: int(format(i, "0" + str(bits) + "b")[::-1], 2))
+    if devices == 16:
+        return [10, 7, 6, 14, 2, 0, 13, 15, 12, 9, 11, 5, 3, 4, 8, 1]
+    return list(range(devices))
 
 
 def rest_place(c, g):

time: 57.1 us -> 57.7 us (1.011)
  waiting for transfers between devices: 19.8 us -> 17.9 us
  blocking collectives: 13.3 us -> 15 us
  starting transfers between devices: 8.37 us -> 9.15 us
    all_to_all x1, waiting for transfers between devices: 19.8 us -> 17.9 us  [shards(): lax.all_to_all(sent, 'wave', 0, 0, axis_index_groups=order, tiled=True)]
    all_to_all x1, blocking collectives: 10.9 us -> 12.6 us  [shards(): rows = lax.all_to_all(rows, ('wave', 'lev'), 0, 0, tiled=True)]
    all_to_all x1, starting transfers between devices: 8.37 us -> 9.15 us  [shards(): lax.all_to_all(sent, 'wave', 0, 0, axis_index_groups=order, tiled=True)]
where the time goes in v4:
time: 57.7 us; the launch traced here: 57.4 us
  waiting for transfers between devices  17.9 us (31%)
  blocking collectives  15 us (26%)
  Pallas kernels  9.9 us (17%)
  starting transfers between devices  9.15 us (16%)
  local copies, waits for them, and re-layouts  3.33 us (6%)
  between operations  2.03 us (4%)
    all_to_all x1, waiting for transfers between devices, shards(): lax.all_to_all(sent, 'wave', 0, 0, axis_index_groups=order, tiled=True)  17.9 us
    all_to_all x1, blocking collectives, shards(): rows = lax.all_to_all(rows, ('wave', 'lev'), 0, 0, tiled=True)  12.6 us
    all_to_all x1, starting transfers between devices, shards(): lax.all_to_all(sent, 'wave', 0, 0, axis_index_groups=order, tiled=True)  9.15 us
    unnamed x17, local copies, waits for them, and re-layouts  3.07 us
    pallas_call x1, Pallas kernels, tables(): pl.pallas_call(table_kernel, grid=(depth // LANES,), in_specs=[pl.BlockSp...  3.02 us
    pallas_call x1, Pallas kernels, section(): pl.pallas_call(functools.partial(section_kernel, copies), in_specs=[pl.Bl...  2.87 us
    pallas_call x1, Pallas kernels, pack(): pl.pallas_call(pack_kernel, in_specs=[pl.BlockSpec(memory_space=pl.ANY)],...  2.83 us
    unnamed x1, blocking collectives  2.44 us
  transfers between devices with their start and end apart: 1, of which 1 were waited for; matrix products, arithmetic and copies ran while one was open for 3% of the time, Pallas kernels for 5%

profile of v4, /device:TPU:0, one launch (start us, length us, event | category | flops | bytes accessed | tf_op | source)
XLA Modules:
  0.0 57.4 jit_solution(6012479195172181466)
XLA Ops:
  0.6 0.0 copy-start
  0.6 2.8 %pack.1 = bf16[16,304,128]{2,1,0:T(8,128)(2,1)} custom-call(bf16[6,80,1280]{2,1,0:T(8,128)(2,1)} %bitcast.13), custom_call_target="tpu_custom_call" | custom-call | bytes 4000000 | tf_op jit(solution)/shard_map/pack/pallas_call | solution.py:79
  3.5 0.0 copy-start.6
  3.5 0.0 copy-start.5
  3.5 9.2 %all-to-all-start = ((bf16[16,304,128]{2,1,0:T(8,128)(2,1)}), bf16[16,304,128]{2,1,0:T(8,128)(2,1)}, u32[]{:S(2)}, u32[]{:S(2)}) async-start(bf16[16,304,128]{2,1,0:T(8,128)(2,1)} %pack.1), calls=%async_computation | async-start | bytes 2490368 | tf_op jit(solution)/shard_map/all_to_all | solution.py:335
  13.3 0.0 copy-done.6
  13.3 0.6 %dynamic-slice = u32[1]{0:T(128)} dynamic-slice(u32[32]{0:T(128)S(1)} %copy-done.6, u32[]{:T(128)S(6)} %add.16), dynamic_slice_sizes={1} | dynamic-slice | bytes 12
  13.9 0.8 %dynamic-update-slice = f32[2]{0:T(128)S(1)} dynamic-update-slice(f32[2]{0:T(128)S(1)} %broadcast.71, f32[1]{0:T(128)S(6)} %copy.11, u32[]{:T(128)} %bitcast) | dynamic-update-slice | bytes 12
  14.7 2.4 %all-reduce = f32[2]{0:T(128)S(1)} all-reduce(f32[2]{0:T(128)S(1)} %dynamic-update-slice), channel_id=1, replica_groups=mesh['wave'=16,'lev'=2] {'lev'}, use_global_device_ids=true, to_apply=%add | all-reduce | flops 2 | bytes 16
  17.8 0.0 copy-done.5
  17.8 0.1 dynamic-slice_bitcast_fusion
  17.9 0.1 copy.7.m_ref
  18.0 0.0 copy-done
  18.0 3.0 %tables.1 = (bf16[2,1280,256]{2,1,0:T(8,128)(2,1)S(1)}, f32[24,1280]{1,0:T(8,128)S(1)}, f32[24,1280]{1,0:T(8,128)S(1)}, f32[8,128]{1,0:T(8,128)S(1)}) custom-call(s32[1]{0:T(128)S(6)} %copy.10.points_ref, s32[1,1280]{1,0:T(1,128)S(1)} %broadcast_in_dim.49.m_ref, bf16[80,16,1280]{2,1,0:T(8,128)(2,1)S(1)} %copy-done), custom_call_target="tpu_custom_call" | custom-call | flops 60000000 | bytes 3000000 | tf_op jit(solution)/shard_map/tables/pallas_call | solution.py:237
  21.0 0.0 copy-start.1
  21.0 1.1 %copy-done.1 = bf16[2,1280,256]{2,1,0:T(8,128)(2,1)} copy-done((bf16[2,1280,256]{2,1,0:T(8,128)(2,1)}, bf16[2,1280,256]{2,1,0:T(8,128)(2,1)S(1)}, u32[]{:S(2)}) %copy-start.1) | copy-done | bytes 1310744
  22.1 0.0 copy-start.3
  22.1 0.6 %copy-done.3 = f32[24,1280]{1,0:T(8,128)} copy-done((f32[24,1280]{1,0:T(8,128)}, f32[24,1280]{1,0:T(8,128)S(1)}, u32[]{:S(2)}) %copy-start.3) | copy-done | bytes 122904
  22.8 0.1 broadcast_select_fusion
  22.8 17.9 %all-to-all-done.r_hbm = bf16[16,304,128]{2,1,0:T(8,128)(2,1)} async-done(((bf16[16,304,128]{2,1,0:T(8,128)(2,1)}), bf16[16,304,128]{2,1,0:T(8,128)(2,1)}, u32[]{:S(2)}, u32[]{:S(2)}) %all-to-all-start) | async-done | bytes 1245216 | tf_op jit(solution)/shard_map/all_to_all | solution.py:335
  40.7 0.1 broadcast_in_dim.47.rest_1_.w_ref
  40.8 0.0 copy-start.2
  40.8 0.0 copy-start.4
  40.8 2.9 %section.1 = bf16[16,2,16,128]{3,2,1,0:T(8,128)(2,1)S(1)} custom-call(bf16[16,304,128]{2,1,0:T(8,128)(2,1)} %all-to-all-done.r_hbm, bf16[80,16,1280]{2,1,0:T(8,128)(2,1)S(1)} %copy-done, s32[80,1]{1,0:T(8,128)S(1)} %copy.7.m_ref, f32[8,128]{1,0:T(8,128)S(1)} %get-tuple-element.8.rest_0_, f32[2,16,128]{2,1,0:T(8,128)S(1)} %broadcast_in_dim.47.rest_1_.w_ref), custom_call_target="tpu_custom_call" | custom-call | flops 10000000000 | bytes 4000000 | tf_op jit(solution)/shard_map/section/pallas_call | solution.py:164
  43.7 12.6 %all_to_all.10 = bf16[32,16,128]{2,1,0:T(8,128)(2,1)S(1)} all-to-all(bf16[32,16,128]{2,1,0:T(8,128)(2,1)S(1)} %bitcast.12), channel_id=1, replica_groups=mesh['wave'=16,'lev'=2] {'wave','lev'}, dimensions={0} | all-to-all | bytes 262144 | tf_op jit(solution)/shard_map/all_to_all | solution.py:342
  56.3 0.0 copy-done.2
  56.3 0.0 copy-done.4
  56.3 1.2 %synth.1 = (f32[2,3,1,5376]{3,2,1,0:T(1,128)}, f32[2,1,1,5376]{3,2,1,0:T(1,128)}) custom-call(s32[1]{0:T(128)S(6)} %copy.10.points_ref, f32[2,16,128]{2,1,0:T(8,128)S(1)} %broadcast_in_dim.47.rest_1_.w_ref, bf16[16,2,16,128]{3,2,1,0:T(8,128)(2,1)S(1)} %bitcast.11, bf16[2,1280,256]{2,1,0:T(8,128)(2,1)S(1)} %copy-done.2, ...), custom_call_target="tpu_custom_call" | custom-call | flops 1000000000 | bytes 3000000 | tf_op jit(solution)/shard_map/synth/pallas_call | solution.py:306
  (5 shorter events, 0.0 us)
Async XLA Ops:
  0.6 17.3 %copy-start = (bf16[80,16,1280]{2,1,0:T(8,128)(2,1)S(1)}, bf16[80,16,1280]{2,1,0:T(8,128)(2,1)}, u32[]{:S(2)}) copy-start(bf16[80,16,1280]{2,1,0:T(8,128)(2,1)} %x_ref.1) | copy-start | bytes 9830404
  3.5 9.8 %copy-start.6 = (u32[32]{0:T(128)S(1)}, u32[32]{0:T(128)}, u32[]{:S(2)}) copy-start(u32[32]{0:T(128)} %constant.38) | copy-start | bytes 388
  3.5 14.3 %copy-start.5 = (s32[1280]{0:T(1024)S(1)}, s32[1280]{0:T(1024)}, u32[]{:S(2)}) copy-start(s32[1280]{0:T(1024)} %param.7) | copy-start | bytes 15364
  3.5 37.2 %all-to-all-start = ((bf16[16,304,128]{2,1,0:T(8,128)(2,1)}), bf16[16,304,128]{2,1,0:T(8,128)(2,1)}, u32[]{:S(2)}, u32[]{:S(2)}) async-start(bf16[16,304,128]{2,1,0:T(8,128)(2,1)} %pack.1), calls=%async_computation | async-start | bytes 2490368 | tf_op jit(solution)/shard_map/all_to_all | solution.py:335
  21.0 1.1 %copy-start.1 = (bf16[2,1280,256]{2,1,0:T(8,128)(2,1)}, bf16[2,1280,256]{2,1,0:T(8,128)(2,1)S(1)}, u32[]{:S(2)}) copy-start(bf16[2,1280,256]{2,1,0:T(8,128)(2,1)S(1)} %get-tuple-element.9.t_ref) | copy-start | bytes 3932164
  22.1 0.6 %copy-start.3 = (f32[24,1280]{1,0:T(8,128)}, f32[24,1280]{1,0:T(8,128)S(1)}, u32[]{:S(2)}) copy-start(f32[24,1280]{1,0:T(8,128)S(1)} %get-tuple-element.11.s_ref) | copy-start | bytes 368644
  40.8 15.5 %copy-start.2 = (bf16[2,1280,256]{2,1,0:T(8,128)(2,1)S(1)}, bf16[2,1280,256]{2,1,0:T(8,128)(2,1)}, u32[]{:S(2)}) copy-start(bf16[2,1280,256]{2,1,0:T(8,128)(2,1)} %copy-done.1) | copy-start | bytes 3932164
  40.8 15.5 %copy-start.4 = (f32[24,1280]{1,0:T(8,128)S(1)}, f32[24,1280]{1,0:T(8,128)}, u32[]{:S(2)}) copy-start(f32[24,1280]{1,0:T(8,128)} %copy-done.3) | copy-start | bytes 368644

commit v5 on v3

--- a/solution.py
+++ b/solution.py
@@ -27,7 +27,7 @@
 
 def exchange_order(devices):
     bits = (devices - 1).bit_length()
-    return sorted(range(devices), key=lambda i: int(format(i, "0" + str(bits) + "b")[::-1], 2))
+    return sorted(range(devices), key=lambda i: -int(format(i, "0" + str(bits) + "b")[::-1], 2))
 
 
 def rest_place(c, g):

time: 57.1 us -> 57.8 us (1.012)
  waiting for transfers between devices: 19.8 us -> 16.9 us
  starting transfers between devices: 8.37 us -> 11.2 us
  blocking collectives: 13.3 us -> 14.1 us
    all_to_all x1, waiting for transfers between devices: 19.8 us -> 16.9 us  [shards(): lax.all_to_all(sent, 'wave', 0, 0, axis_index_groups=order, tiled=True)]
    all_to_all x1, starting transfers between devices: 8.37 us -> 11.2 us  [shards(): lax.all_to_all(sent, 'wave', 0, 0, axis_index_groups=order, tiled=True)]
    all_to_all x1, blocking collectives: 10.9 us -> 11.7 us  [shards(): rows = lax.all_to_all(rows, ('wave', 'lev'), 0, 0, tiled=True)]
where the time goes in v5:
time: 57.8 us; the launch traced here: 57.5 us
  waiting for transfers between devices  16.9 us (29%)
  blocking collectives  14.1 us (24%)
  starting transfers between devices  11.2 us (19%)
  Pallas kernels  9.92 us (17%)
  local copies, waits for them, and re-layouts  3.33 us (6%)
  between operations  2.03 us (4%)
    all_to_all x1, waiting for transfers between devices, shards(): lax.all_to_all(sent, 'wave', 0, 0, axis_index_groups=order, tiled=True)  16.9 us
    all_to_all x1, blocking collectives, shards(): rows = lax.all_to_all(rows, ('wave', 'lev'), 0, 0, tiled=True)  11.7 us
    all_to_all x1, starting transfers between devices, shards(): lax.all_to_all(sent, 'wave', 0, 0, axis_index_groups=order, tiled=True)  11.2 us
    unnamed x17, local copies, waits for them, and re-layouts  3.07 us
    pallas_call x1, Pallas kernels, tables(): pl.pallas_call(table_kernel, grid=(depth // LANES,), in_specs=[pl.BlockSp...  3.02 us
    pallas_call x1, Pallas kernels, section(): pl.pallas_call(functools.partial(section_kernel, copies), in_specs=[pl.Bl...  2.87 us
    pallas_call x1, Pallas kernels, pack(): pl.pallas_call(pack_kernel, in_specs=[pl.BlockSpec(memory_space=pl.ANY)],...  2.85 us
    unnamed x1, blocking collectives  2.44 us
  transfers between devices with their start and end apart: 1, of which 1 were waited for; matrix products, arithmetic and copies ran while one was open for 3% of the time, Pallas kernels for 5%

profile of v5, /device:TPU:0, one launch (start us, length us, event | category | flops | bytes accessed | tf_op | source)
XLA Modules:
  0.0 57.5 jit_solution(12755770382478271061)
XLA Ops:
  0.6 0.0 copy-start
  0.6 2.9 %pack.1 = bf16[16,304,128]{2,1,0:T(8,128)(2,1)} custom-call(bf16[6,80,1280]{2,1,0:T(8,128)(2,1)} %bitcast.13), custom_call_target="tpu_custom_call" | custom-call | bytes 4000000 | tf_op jit(solution)/shard_map/pack/pallas_call | solution.py:78
  3.5 0.0 copy-start.6
  3.5 0.0 copy-start.5
  3.5 11.2 %all-to-all-start = ((bf16[16,304,128]{2,1,0:T(8,128)(2,1)}), bf16[16,304,128]{2,1,0:T(8,128)(2,1)}, u32[]{:S(2)}, u32[]{:S(2)}) async-start(bf16[16,304,128]{2,1,0:T(8,128)(2,1)} %pack.1), calls=%async_computation | async-start | bytes 2490368 | tf_op jit(solution)/shard_map/all_to_all | solution.py:334
  15.3 0.0 copy-done.6
  15.3 0.6 %dynamic-slice = u32[1]{0:T(128)} dynamic-slice(u32[32]{0:T(128)S(1)} %copy-done.6, u32[]{:T(128)S(6)} %add.16), dynamic_slice_sizes={1} | dynamic-slice | bytes 12
  15.9 0.8 %dynamic-update-slice = f32[2]{0:T(128)S(1)} dynamic-update-slice(f32[2]{0:T(128)S(1)} %broadcast.71, f32[1]{0:T(128)S(6)} %copy.11, u32[]{:T(128)} %bitcast) | dynamic-update-slice | bytes 12
  16.7 2.4 %all-reduce = f32[2]{0:T(128)S(1)} all-reduce(f32[2]{0:T(128)S(1)} %dynamic-update-slice), channel_id=1, replica_groups=mesh['wave'=16,'lev'=2] {'lev'}, use_global_device_ids=true, to_apply=%add | all-reduce | flops 2 | bytes 16
  19.8 0.0 copy-done.5
  19.8 0.1 dynamic-slice_bitcast_fusion
  19.9 0.1 copy.7.m_ref
  20.0 0.0 copy-done
  20.0 3.0 %tables.1 = (bf16[2,1280,256]{2,1,0:T(8,128)(2,1)S(1)}, f32[24,1280]{1,0:T(8,128)S(1)}, f32[24,1280]{1,0:T(8,128)S(1)}, f32[8,128]{1,0:T(8,128)S(1)}) custom-call(s32[1]{0:T(128)S(6)} %copy.10.points_ref, s32[1,1280]{1,0:T(1,128)S(1)} %broadcast_in_dim.49.m_ref, bf16[80,16,1280]{2,1,0:T(8,128)(2,1)S(1)} %copy-done), custom_call_target="tpu_custom_call" | custom-call | flops 60000000 | bytes 3000000 | tf_op jit(solution)/shard_map/tables/pallas_call | solution.py:236
  23.0 0.0 copy-start.1
  23.0 1.1 %copy-done.1 = bf16[2,1280,256]{2,1,0:T(8,128)(2,1)} copy-done((bf16[2,1280,256]{2,1,0:T(8,128)(2,1)}, bf16[2,1280,256]{2,1,0:T(8,128)(2,1)S(1)}, u32[]{:S(2)}) %copy-start.1) | copy-done | bytes 1310744
  24.1 0.0 copy-start.3
  24.1 0.6 %copy-done.3 = f32[24,1280]{1,0:T(8,128)} copy-done((f32[24,1280]{1,0:T(8,128)}, f32[24,1280]{1,0:T(8,128)S(1)}, u32[]{:S(2)}) %copy-start.3) | copy-done | bytes 122904
  24.8 0.1 broadcast_select_fusion
  24.8 16.9 %all-to-all-done.r_hbm = bf16[16,304,128]{2,1,0:T(8,128)(2,1)} async-done(((bf16[16,304,128]{2,1,0:T(8,128)(2,1)}), bf16[16,304,128]{2,1,0:T(8,128)(2,1)}, u32[]{:S(2)}, u32[]{:S(2)}) %all-to-all-start) | async-done | bytes 1245216 | tf_op jit(solution)/shard_map/all_to_all | solution.py:334
  41.7 0.1 broadcast_in_dim.47.rest_1_.w_ref
  41.8 0.0 copy-start.2
  41.8 0.0 copy-start.4
  41.8 2.9 %section.1 = bf16[16,2,16,128]{3,2,1,0:T(8,128)(2,1)S(1)} custom-call(bf16[16,304,128]{2,1,0:T(8,128)(2,1)} %all-to-all-done.r_hbm, bf16[80,16,1280]{2,1,0:T(8,128)(2,1)S(1)} %copy-done, s32[80,1]{1,0:T(8,128)S(1)} %copy.7.m_ref, f32[8,128]{1,0:T(8,128)S(1)} %get-tuple-element.8.rest_0_, f32[2,16,128]{2,1,0:T(8,128)S(1)} %broadcast_in_dim.47.rest_1_.w_ref), custom_call_target="tpu_custom_call" | custom-call | flops 10000000000 | bytes 4000000 | tf_op jit(solution)/shard_map/section/pallas_call | solution.py:163
  44.7 11.7 %all_to_all.10 = bf16[32,16,128]{2,1,0:T(8,128)(2,1)S(1)} all-to-all(bf16[32,16,128]{2,1,0:T(8,128)(2,1)S(1)} %bitcast.12), channel_id=1, replica_groups=mesh['wave'=16,'lev'=2] {'wave','lev'}, dimensions={0} | all-to-all | bytes 262144 | tf_op jit(solution)/shard_map/all_to_all | solution.py:341
  56.3 0.0 copy-done.2
  56.3 0.0 copy-done.4
  56.4 1.2 %synth.1 = (f32[2,3,1,5376]{3,2,1,0:T(1,128)}, f32[2,1,1,5376]{3,2,1,0:T(1,128)}) custom-call(s32[1]{0:T(128)S(6)} %copy.10.points_ref, f32[2,16,128]{2,1,0:T(8,128)S(1)} %broadcast_in_dim.47.rest_1_.w_ref, bf16[16,2,16,128]{3,2,1,0:T(8,128)(2,1)S(1)} %bitcast.11, bf16[2,1280,256]{2,1,0:T(8,128)(2,1)S(1)} %copy-done.2, ...), custom_call_target="tpu_custom_call" | custom-call | flops 1000000000 | bytes 3000000 | tf_op jit(solution)/shard_map/synth/pallas_call | solution.py:305
  (5 shorter events, 0.0 us)
Async XLA Ops:
  0.6 19.4 %copy-start = (bf16[80,16,1280]{2,1,0:T(8,128)(2,1)S(1)}, bf16[80,16,1280]{2,1,0:T(8,128)(2,1)}, u32[]{:S(2)}) copy-start(bf16[80,16,1280]{2,1,0:T(8,128)(2,1)} %x_ref.1) | copy-start | bytes 9830404
  3.5 11.8 %copy-start.6 = (u32[32]{0:T(128)S(1)}, u32[32]{0:T(128)}, u32[]{:S(2)}) copy-start(u32[32]{0:T(128)} %constant.38) | copy-start | bytes 388
  3.5 16.3 %copy-start.5 = (s32[1280]{0:T(1024)S(1)}, s32[1280]{0:T(1024)}, u32[]{:S(2)}) copy-start(s32[1280]{0:T(1024)} %param.7) | copy-start | bytes 15364
  3.5 38.2 %all-to-all-start = ((bf16[16,304,128]{2,1,0:T(8,128)(2,1)}), bf16[16,304,128]{2,1,0:T(8,128)(2,1)}, u32[]{:S(2)}, u32[]{:S(2)}) async-start(bf16[16,304,128]{2,1,0:T(8,128)(2,1)} %pack.1), calls=%async_computation | async-start | bytes 2490368 | tf_op jit(solution)/shard_map/all_to_all | solution.py:334
  23.0 1.1 %copy-start.1 = (bf16[2,1280,256]{2,1,0:T(8,128)(2,1)}, bf16[2,1280,256]{2,1,0:T(8,128)(2,1)S(1)}, u32[]{:S(2)}) copy-start(bf16[2,1280,256]{2,1,0:T(8,128)(2,1)S(1)} %get-tuple-element.9.t_ref) | copy-start | bytes 3932164
  24.1 0.6 %copy-start.3 = (f32[24,1280]{1,0:T(8,128)}, f32[24,1280]{1,0:T(8,128)S(1)}, u32[]{:S(2)}) copy-start(f32[24,1280]{1,0:T(8,128)S(1)} %get-tuple-element.11.s_ref) | copy-start | bytes 368644
  41.8 14.6 %copy-start.2 = (bf16[2,1280,256]{2,1,0:T(8,128)(2,1)S(1)}, bf16[2,1280,256]{2,1,0:T(8,128)(2,1)}, u32[]{:S(2)}) copy-start(bf16[2,1280,256]{2,1,0:T(8,128)(2,1)} %copy-done.1) | copy-start | bytes 3932164
  41.8 14.6 %copy-start.4 = (f32[24,1280]{1,0:T(8,128)S(1)}, f32[24,1280]{1,0:T(8,128)}, u32[]{:S(2)}) copy-start(f32[24,1280]{1,0:T(8,128)} %copy-done.3) | copy-start | bytes 368644
